TPU v7x, 32 devices: a whole 2x2x4 slice. The times are simulated.
32 devices in a mesh: pp: 4 (over y, x), ep: 8 (over z, core).
Axes of the slice: x: 2, y: 2, z: 4, core: 2. Of those that a mesh axis runs over, the one named last changes fastest.
Arguments:
- prev_out: bfloat16 [4, 1024, 7168], P('pp', 'ep'), may hold values from -6 to 6
- fwd_experts: int32 [4, 1024, 2], P('pp', 'ep'), may hold values from 0 to 3, all different within a row; in each aligned block of 128 rows (0 to 127, 128 to 255, ..., all dimensions but the last counted through in order) at most 96 rows name the same one
- expert_weights: bfloat16 [4, 8, 7168, 1024], P('pp', 'ep'), may hold values from -0.0625 to 0.0625
- bwd_experts: int32 [4, 1024, 2], P('pp', 'ep'), may hold values from 0 to 3, all different within a row; in each aligned block of 128 rows (0 to 127, 128 to 255, ..., all dimensions but the last counted through in order) at most 96 rows name the same one
- grad_hidden: bfloat16 [4, 8, 8, 96, 512], P('pp', 'ep'), may hold values from -6 to 6
- saved_pre: bfloat16 [4, 8, 8, 96, 1024], P('pp', 'ep'), may hold values from -6 to 6
Outputs:
- hidden_out: bfloat16 [4, 8, 8, 96, 512], P('pp', 'ep')
- grad_rows: bfloat16 [4, 1024, 7168], P('pp', 'ep')
Inputs may be any that keep to these rules, and one draw needn't show every extreme that they name: `fwd_experts`: each row names 2 different experts, and within the 128 rows of one device no expert is named more than 96 times. `bwd_experts`: each row names 2 different experts, and within the 128 rows of one device no expert is named more than 96 times.
All inputs are finite; a program needn't handle non-finite values.
Results may differ from a plain program's by a relative error of at most 0.0066.
Values may be sent and summed in bfloat16 or wider, within the bound.
A program may use at most 128 MiB of HBM per device.

v0:
```python
import jax
import jax.numpy as jnp
from jax import lax
from jax.sharding import PartitionSpec as P


def shifted(block, axis, distance):
    devices = range(lax.axis_size(axis))
    route = [((i - distance) % len(devices), i) for i in devices]
    return lax.ppermute(block, axis, route)


def partner_2(value, axis, bit):
    mask = 2**bit
    pairs = [(source, source ^ mask) for source in range(lax.axis_size(axis))]
    return lax.ppermute(value, axis, pairs)


def slot_table(route_ids, expert_count, capacity):
    token_count, choice_count = route_ids.shape
    flattened = route_ids.reshape(token_count * choice_count)
    onehot = (flattened[:, None] == jnp.arange(expert_count, dtype=jnp.int32)[None, :]).astype(
        jnp.int32
    )
    earlier = jnp.cumsum(onehot, axis=0) - onehot
    slot_index = jnp.sum(earlier * onehot, axis=1)
    slot_match = (slot_index[:, None] == jnp.arange(capacity, dtype=jnp.int32)[None, :]).astype(
        jnp.float32
    )
    expert_match = onehot.astype(jnp.float32)
    joined = jnp.einsum("re,rc->rec", expert_match, slot_match).reshape(
        token_count, choice_count, expert_count, capacity
    )
    return jnp.transpose(jnp.sum(joined, axis=1), (1, 2, 0))


def swiglu_backward(upstream, saved):
    hid_units = upstream.shape[-1]
    pre_float = saved.astype(jnp.float32)
    gate_pre = pre_float[..., :hid_units]
    up_pre = pre_float[..., hid_units:]
    sigmoid_gate = jax.nn.sigmoid(gate_pre)
    upstream_float = upstream.astype(jnp.float32)
    grad_gate = upstream_float * up_pre * sigmoid_gate * (1.0 + gate_pre * (1.0 - sigmoid_gate))
    grad_up = upstream_float * gate_pre * sigmoid_gate
    return jnp.concatenate([grad_gate, grad_up], axis=-1).astype(jnp.bfloat16)


def shards(prev_out, fwd_experts, expert_weights, bwd_experts, grad_hidden, saved_pre):
    groups = lax.axis_size("ep")
    experts = groups // 2
    capacity = grad_hidden.shape[3]
    hid_units = grad_hidden.shape[4]
    model_width = prev_out.shape[2]
    half_width = model_width // 2
    weights = expert_weights[0, 0]
    even_side = lax.axis_index("ep") % 2 == 0
    section_rows = shifted(prev_out[0], "pp", 1)
    fwd_table = slot_table(fwd_experts[0], experts, capacity).astype(jnp.bfloat16)
    picked = jnp.einsum(
        "ect,td->ecd", fwd_table, section_rows, preferred_element_type=jnp.float32
    ).astype(jnp.bfloat16)
    outgoing = jnp.stack([picked[..., :half_width], picked[..., half_width:]], axis=1).reshape(
        groups, capacity, half_width
    )
    received = lax.all_to_all(outgoing, "ep", split_axis=0, concat_axis=0, tiled=True)
    partner = partner_2(received, "ep", 0)
    leading = jnp.where(even_side, received, partner)
    trailing = jnp.where(even_side, partner, received)
    projected = jnp.einsum(
        "scd,dh->sch",
        jnp.concatenate([leading, trailing], axis=2),
        weights,
        preferred_element_type=jnp.float32,
    )
    hidden = (jax.nn.silu(projected[..., :hid_units]) * projected[..., hid_units:]).astype(
        jnp.bfloat16
    )
    grad_pre = swiglu_backward(grad_hidden[0, 0], saved_pre[0, 0])
    partial_rows = jnp.einsum(
        "sch,dh->scd", grad_pre, weights, preferred_element_type=jnp.float32
    ).astype(jnp.bfloat16)
    bwd_table = slot_table(bwd_experts[0], experts, capacity).astype(jnp.bfloat16)
    own_half = jnp.where(even_side, partial_rows[..., :half_width], partial_rows[..., half_width:])
    other_half = jnp.where(
        even_side, partial_rows[..., half_width:], partial_rows[..., :half_width]
    )
    received = partner_2(other_half, "ep", 0)
    pair_half = (own_half.astype(jnp.float32) + received.astype(jnp.float32)).astype(jnp.bfloat16)
    returned = lax.all_to_all(pair_half, "ep", split_axis=0, concat_axis=0, tiled=True)
    halves = returned.reshape(experts, 2, capacity, half_width)
    summed = jnp.concatenate([halves[:, 0], halves[:, 1]], axis=2)
    grad_in = jnp.einsum(
        "ect,ecd->td", bwd_table, summed, preferred_element_type=jnp.float32
    ).astype(jnp.bfloat16)
    grad_rows = shifted(grad_in, "pp", -1)
    return (hidden[None, None], grad_rows[None])


def solution(mesh):
    placed = (
        P("pp", "ep", None),
        P("pp", "ep", None),
        P("pp", "ep", None, None),
        P("pp", "ep", None),
        P("pp", "ep", None, None, None),
        P("pp", "ep", None, None, None),
    )
    return jax.shard_map(
        shards,
        mesh=mesh,
        in_specs=placed,
        out_specs=(P("pp", "ep", None, None, None), P("pp", "ep", None)),
        check_vma=False,
    )
```

profile of v0, /device:TPU:0, one launch (start us, length us, event | category | flops | bytes accessed | tf_op | source)
XLA Modules:
  0.0 354.1 jit_solution(10471346471250098798)
XLA Ops:
  0.6 3.0 collective-permute-start
  3.6 0.8 copy.42
  4.4 0.1 eq.86
  4.6 0.1 eq.82
  4.7 1.2 reduce-window.14
  5.9 0.1 slice.58
  6.0 0.1 copy.44
  6.1 0.1 copy.45
  6.3 0.1 fusion.25
  6.5 0.2 broadcast_multiply_fusion.1
  6.7 0.8 reduce_sum.37
  7.4 0.1 copy.55
  7.6 1.8 bitcast_convert_fusion
  9.4 1.9 fusion.17
  11.3 33.5 %collective-permute-done = bf16[128,7168]{1,0:T(8,128)(2,1)S(1)} collective-permute-done((bf16[128,7168]{1,0:T(8,128)(2,1)}, bf16[128,7168]{1,0:T(8,128)(2,1)S(1)}, u32[]{:S(2)}, u32[]{:S(2)}) %collective-permute-start) | collective-permute-done | bytes 1835040 | tf_op jit(solution)/shard_map/ppermute | solution.py:10
  44.8 1.6 convolution_convert_fusion
  46.4 0.5 slice_bitcast_fusion.3
  46.9 0.5 pad_maximum_fusion
  47.4 2.7 copy.47
  50.2 5.2 %all-to-all-start = ((bf16[8,96,3584]{2,1,0:T(8,128)(2,1)}), bf16[8,96,3584]{2,1,0:T(8,128)(2,1)}, u32[]{:S(2)}, u32[]{:S(2)}) async-start(bf16[8,96,3584]{2,1,0:T(8,128)(2,1)} %bitcast.71), calls=%async_computation | async-start | bytes 11010048 | tf_op jit(solution)/shard_map/all_to_all | solution.py:66
  55.4 19.0 %fusion.4 = bf16[8,96,7168]{2,1,0:T(8,128)(2,1)} fusion(bf16[1,1,7168,1024]{3,2,1,0:T(8,128)(2,1)} %param.8, bf16[8,96,512]{2,1,0:T(8,128)(2,1)S(1)} %copy-done.3, bf16[8,96,512]{2,1,0:T(8,128)(2,1)S(1)} %copy-done.2), kind=kOutput, calls=%fused_computation.4 | convolution fusion | flops 11282939904 | bytes 27262976 | tf_op jit(solution)/shard_map/sch,dh->scd/dot_general | solution.py:80
  74.4 7.7 %broadcast_select_fusion = bf16[8,96,3584]{2,1,0:T(8,128)(2,1)} fusion(pred[]{:T(512)S(6)} %eq.81, bf16[8,96,7168]{2,1,0:T(8,128)(2,1)} %fusion.4), kind=kLoop, calls=%fused_computation.16 | loop fusion | flops 2752512 | bytes 16515073 | tf_op jit(solution)/shard_map/jit(_where)/select_n | solution.py:85
  82.1 0.5 collective-permute-start.2
  82.6 8.9 %collective-permute-done.2 = bf16[8,96,3584]{2,1,0:T(8,128)(2,1)S(1)} collective-permute-done((bf16[8,96,3584]{2,1,0:T(8,128)(2,1)}, bf16[8,96,3584]{2,1,0:T(8,128)(2,1)S(1)}, u32[]{:S(2)}, u32[]{:S(2)}) %collective-permute-start.2) | collective-permute-done | bytes 5505056 | tf_op jit(solution)/shard_map/ppermute | solution.py:16
  91.5 4.2 %add_convert_fusion = bf16[8,96,3584]{2,1,0:T(8,128)(2,1)} fusion(bf16[8,96,3584]{2,1,0:T(8,128)(2,1)S(1)} %collective-permute-done.2, pred[]{:T(512)S(6)} %eq.81, bf16[8,96,7168]{2,1,0:T(8,128)(2,1)S(1)} %copy-done), kind=kLoop, calls=%fused_computation.8 | loop fusion | flops 13762560 | bytes 22020096 | tf_op jit(solution)/shard_map/convert_element_type | solution.py:89
  95.7 81.9 %all-to-all-done = bf16[8,96,3584]{2,1,0:T(8,128)(2,1)} async-done(((bf16[8,96,3584]{2,1,0:T(8,128)(2,1)}), bf16[8,96,3584]{2,1,0:T(8,128)(2,1)}, u32[]{:S(2)}, u32[]{:S(2)}) %all-to-all-start) | async-done | bytes 5505056 | tf_op jit(solution)/shard_map/all_to_all | solution.py:66
  177.6 4.9 %all-to-all-start.1 = ((bf16[8,96,3584]{2,1,0:T(8,128)(2,1)}), bf16[8,96,3584]{2,1,0:T(8,128)(2,1)}, u32[]{:S(2)}, u32[]{:S(2)}) async-start(bf16[8,96,3584]{2,1,0:T(8,128)(2,1)} %add_convert_fusion), calls=%async_computation.1 | async-start | bytes 11010048 | tf_op jit(solution)/shard_map/all_to_all | solution.py:90
  182.4 0.2 collective-permute-start.1
  182.6 0.1 copy.48
  182.8 0.1 eq.97
  182.9 0.1 eq.93
  183.0 1.2 reduce-window.16
  184.3 0.1 slice.63
  184.3 0.1 copy.50
  184.5 0.1 copy.51
  184.7 0.1 fusion.26
  184.8 0.2 broadcast_multiply_fusion
  185.0 0.8 reduce_sum.39
  185.8 0.1 copy.56
  185.9 118.5 %all-to-all-done.1 = bf16[8,96,3584]{2,1,0:T(8,128)(2,1)} async-done(((bf16[8,96,3584]{2,1,0:T(8,128)(2,1)}), bf16[8,96,3584]{2,1,0:T(8,128)(2,1)}, u32[]{:S(2)}, u32[]{:S(2)}) %all-to-all-start.1) | async-done | bytes 5505056 | tf_op jit(solution)/shard_map/all_to_all | solution.py:90
  304.4 3.0 slice_bitcast_fusion.1
  307.3 3.8 %fusion.10 = bf16[128,7168]{1,0:T(8,128)(2,1)} fusion(bf16[4,96,3584]{2,1,0:T(8,128)(2,1)S(1)} %get-tuple-element.5, bf16[4,96,3584]{2,1,0:T(8,128)(2,1)S(1)} %get-tuple-element.4, bf16[128,4,96]{0,2,1:T(8,128)(2,1)S(1)} %copy.56), kind=kOutput, calls=%fused_computation.11 | convolution fusion | flops 716570624 | bytes 7438336 | tf_op jit(solution)/shard_map/ect,ecd->td/dot_general | solution.py:93
  311.1 1.6 collective-permute-start.3
  312.7 9.0 %broadcast_select_fusion.2 = (bf16[8,96,3584]{2,1,0:T(8,128)(2,1)}, bf16[8,96,3584]{2,1,0:T(8,128)(2,1)}) fusion(bf16[8,96,3584]{2,1,0:T(8,128)(2,1)} %all-to-all-done, bf16[8,96,3584]{2,1,0:T(8,128)(2,1)} %collective-permute-done.1, pred[]{:T(512)S(6)} %eq.81), kind=kLoop, calls=%fused_computation.18 | loop fusion | flops 5505024 | bytes 22020096 | tf_op jit(solution)/shard_map/jit(_where)/select_n | solution.py:68
  321.6 18.2 %fusion.2 = f32[8,96,1024]{2,1,0:T(8,128)S(1)} fusion(bf16[1,1,7168,1024]{3,2,1,0:T(8,128)(2,1)} %param.8, bf16[8,96,3584]{2,1,0:T(8,128)(2,1)} %get-tuple-element.3, bf16[8,96,3584]{2,1,0:T(8,128)(2,1)} %get-tuple-element.2), kind=kOutput, calls=%fused_computation.2 | convolution fusion | flops 11296309248 | bytes 28835840 | tf_op jit(solution)/shard_map/scd,dh->sch/dot_general | solution.py:70
  339.8 1.4 fusion.24
  341.2 11.7 %collective-permute-done.3 = bf16[128,7168]{1,0:T(8,128)(2,1)S(1)} collective-permute-done((bf16[128,7168]{1,0:T(8,128)(2,1)}, bf16[128,7168]{1,0:T(8,128)(2,1)S(1)}, u32[]{:S(2)}, u32[]{:S(2)}) %collective-permute-start.3) | collective-permute-done | bytes 1835040 | tf_op jit(solution)/shard_map/ppermute | solution.py:10
  352.9 1.2 copy.64
  (23 shorter events, 0.3 us)
Async XLA Ops:
  0.6 44.2 %collective-permute-start = (bf16[128,7168]{1,0:T(8,128)(2,1)}, bf16[128,7168]{1,0:T(8,128)(2,1)S(1)}, u32[]{:S(2)}, u32[]{:S(2)}) collective-permute-start(bf16[128,7168]{1,0:T(8,128)(2,1)} %bitcast.77), channel_id=1, source_target_pairs={{24,0},{0,8},{8,16},{16,24},{25,1},{1,9},{9,17},{17,25},{26,2},{2,... | collective-permute-start | bytes 5505032 | tf_op jit(solution)/shard_map/ppermute | solution.py:10
  6.5 2.9 copy-start.1
  50.2 5.2 %copy-start.2 = (bf16[8,96,512]{2,1,0:T(8,128)(2,1)S(1)}, bf16[8,96,512]{2,1,0:T(8,128)(2,1)}, u32[]{:S(2)}) copy-start(bf16[8,96,512]{2,1,0:T(8,128)(2,1)} %get-tuple-element.8) | copy-start | bytes 2359300
  50.2 5.2 %copy-start.3 = (bf16[8,96,512]{2,1,0:T(8,128)(2,1)S(1)}, bf16[8,96,512]{2,1,0:T(8,128)(2,1)}, u32[]{:S(2)}) copy-start(bf16[8,96,512]{2,1,0:T(8,128)(2,1)} %get-tuple-element.9) | copy-start | bytes 2359300
  50.2 127.4 %all-to-all-start = ((bf16[8,96,3584]{2,1,0:T(8,128)(2,1)}), bf16[8,96,3584]{2,1,0:T(8,128)(2,1)}, u32[]{:S(2)}, u32[]{:S(2)}) async-start(bf16[8,96,3584]{2,1,0:T(8,128)(2,1)} %bitcast.71), calls=%async_computation | async-start | bytes 11010048 | tf_op jit(solution)/shard_map/all_to_all | solution.py:66
  74.4 17.1 %copy-start = (bf16[8,96,7168]{2,1,0:T(8,128)(2,1)S(1)}, bf16[8,96,7168]{2,1,0:T(8,128)(2,1)}, u32[]{:S(2)}) copy-start(bf16[8,96,7168]{2,1,0:T(8,128)(2,1)} %fusion.4) | copy-start | bytes 33030148
  82.1 9.4 %collective-permute-start.2 = (bf16[8,96,3584]{2,1,0:T(8,128)(2,1)}, bf16[8,96,3584]{2,1,0:T(8,128)(2,1)S(1)}, u32[]{:S(2)}, u32[]{:S(2)}) collective-permute-start(bf16[8,96,3584]{2,1,0:T(8,128)(2,1)} %broadcast_select_fusion), channel_id=1, source_target_pairs={{0,1},{1,0},{2,3},{3,2},{4,5},{5,4},{6,7},{7,6},{8,9},{9,8},{10,11... | collective-permute-start | bytes 16515080 | tf_op jit(solution)/shard_map/ppermute | solution.py:16
  95.7 87.0 %copy-start.4 = (s32[1,128,2]{1,2,0:T(2,128)S(1)}, s32[1,128,2]{1,2,0:T(2,128)}, u32[]{:S(2)}) copy-start(s32[1,128,2]{1,2,0:T(2,128)} %param.9) | copy-start | bytes 3076
  177.6 126.8 %all-to-all-start.1 = ((bf16[8,96,3584]{2,1,0:T(8,128)(2,1)}), bf16[8,96,3584]{2,1,0:T(8,128)(2,1)}, u32[]{:S(2)}, u32[]{:S(2)}) async-start(bf16[8,96,3584]{2,1,0:T(8,128)(2,1)} %add_convert_fusion), calls=%async_computation.1 | async-start | bytes 11010048 | tf_op jit(solution)/shard_map/all_to_all | solution.py:90
  182.4 130.2 %collective-permute-start.1 = (bf16[8,96,3584]{2,1,0:T(8,128)(2,1)}, bf16[8,96,3584]{2,1,0:T(8,128)(2,1)}, u32[]{:S(2)}, u32[]{:S(2)}) collective-permute-start(bf16[8,96,3584]{2,1,0:T(8,128)(2,1)} %all-to-all-done), channel_id=1, source_target_pairs={{0,1},{1,0},{2,3},{3,2},{4,5},{5,4},{6,7},{7,6},{8,9},{9,8},{10,11... | collective-permute-start | bytes 16515080 | tf_op jit(solution)/shard_map/ppermute | solution.py:16
  311.1 41.8 %collective-permute-start.3 = (bf16[128,7168]{1,0:T(8,128)(2,1)}, bf16[128,7168]{1,0:T(8,128)(2,1)S(1)}, u32[]{:S(2)}, u32[]{:S(2)}) collective-permute-start(bf16[128,7168]{1,0:T(8,128)(2,1)} %fusion.10), channel_id=1, source_target_pairs={{8,0},{16,8},{24,16},{0,24},{9,1},{17,9},{25,17},{1,25},{10,2},{18... | collective-permute-start | bytes 5505032 | tf_op jit(solution)/shard_map/ppermute | solution.py:10
where the time goes:
time: 354 us
  waiting for transfers between devices  254 us (72%)
  matrix products  42.6 us (12%)
  other arithmetic  31.2 us (9%)
  starting transfers between devices  15.3 us (4%)
  local copies, waits for them, and re-layouts  9.71 us (3%)
    all_to_all x1, waiting for transfers between devices, shards(): lax.all_to_all(pair_half, 'ep', split_axis=0, concat_axis=0, tiled=True)  118 us
    all_to_all x1, waiting for transfers between devices, shards(): lax.all_to_all(outgoing, 'ep', split_axis=0, concat_axis=0, tiled=True)  81.9 us
    ppermute x2, waiting for transfers between devices, shifted(): return lax.ppermute(block, axis, route)  45.2 us
    dot_general x1, matrix products, shards(): jnp.einsum('sch,dh->scd', grad_pre, weights, preferred_element_type=jnp.f...  19 us
    dot_general x1, matrix products, shards(): jnp.einsum('scd,dh->sch', jnp.concatenate([leading, trailing], axis=2), w...  18.2 us
    select_n x1, other arithmetic, shards(): leading = jnp.where(even_side, received, partner)  8.95 us
    ppermute x2, waiting for transfers between devices, partner_2(): return lax.ppermute(value, axis, pairs)  8.87 us
    select_n x1, other arithmetic, shards(): jnp.where(even_side, partial_rows[..., half_width:], partial_rows[..., :h...  7.7 us
  transfers between devices with their start and end apart: 6, of which 5 were waited for; matrix products, arithmetic and copies ran while one was open for 22% of the time, Pallas kernels for 0%

commit v1 on v0

v1 whole, which is shorter than its diff:
```python
import jax
import jax.numpy as jnp
from jax import lax
from jax.sharding import PartitionSpec as P

PARTS = 2


def shifted(block, axis, distance):
    devices = range(lax.axis_size(axis))
    route = [((i - distance) % len(devices), i) for i in devices]
    return lax.ppermute(block, axis, route)


def partner_of(value):
    pairs = [(i, i ^ 1) for i in range(lax.axis_size("ep"))]
    return lax.ppermute(value, "ep", pairs)


def step_along(value, first, last, way):
    pairs = [(2 * z + c, 2 * (z + way) + c) for z in range(first, last + 1) for c in range(2)]
    return lax.ppermute(value, "ep", pairs)


def slots_of(route_ids, expert, capacity):
    named = jnp.any(route_ids == expert, axis=2).astype(jnp.int32)
    slot = jnp.cumsum(named, axis=1) - 1
    place = jnp.where(named == 1, slot, -1)
    return (place[:, None, :] == jnp.arange(capacity, dtype=jnp.int32)[None, :, None]).astype(
        jnp.bfloat16
    )


def swiglu_backward(upstream, saved):
    hid_units = upstream.shape[-1]
    pre_float = saved.astype(jnp.float32)
    gate_pre = pre_float[..., :hid_units]
    up_pre = pre_float[..., hid_units:]
    sigmoid_gate = jax.nn.sigmoid(gate_pre)
    upstream_float = upstream.astype(jnp.float32)
    grad_gate = upstream_float * up_pre * sigmoid_gate * (1.0 + gate_pre * (1.0 - sigmoid_gate))
    grad_up = upstream_float * gate_pre * sigmoid_gate
    return jnp.concatenate([grad_gate, grad_up], axis=-1).astype(jnp.bfloat16)


def shards(prev_out, fwd_experts, expert_weights, bwd_experts, grad_hidden, saved_pre):
    groups = lax.axis_size("ep")
    chips = groups // 2
    capacity = grad_hidden.shape[3]
    hid_units = grad_hidden.shape[4]
    width = prev_out.shape[2]
    part = width // PARTS
    weights = expert_weights[0, 0]
    me = lax.axis_index("ep")
    z, core = me // 2, me % 2
    tokens, top = fwd_experts.shape[1:]

    routes = lax.all_gather(
        jnp.concatenate([fwd_experts[0], bwd_experts[0]], axis=1), "ep", axis=0
    )
    fwd_pick = slots_of(routes[..., :top], z, capacity)
    bwd_pick = slots_of(routes[..., top:], z, capacity)
    fwd_own = lax.dynamic_index_in_dim(
        fwd_pick.reshape(chips, 2, capacity, tokens), core, 1, keepdims=False
    )
    bwd_own = lax.dynamic_index_in_dim(
        bwd_pick.reshape(chips, 2, capacity, tokens), core, 1, keepdims=False
    )

    grad_pre = swiglu_backward(grad_hidden[0, 0], saved_pre[0, 0])
    by_core = grad_pre.reshape(chips, 2, capacity, 2 * hid_units)
    grad_own = lax.dynamic_index_in_dim(by_core, core, 1, keepdims=False)
    grad_other = lax.dynamic_index_in_dim(by_core, 1 - core, 1, keepdims=False)

    projected_own = 0.0
    projected_other = 0.0
    grad_rows = []
    for k in range(PARTS):
        columns = slice(k * part, (k + 1) * part)
        own_weights = weights[columns]

        rows = shifted(prev_out[0, :, columns], "pp", 1)
        below, above = [], []
        up = down = rows
        for hop in range(1, chips):
            up = step_along(up, hop - 1, chips - 2, 1)
            down = step_along(down, 1, chips - hop, -1)
            below.insert(0, up)
            above.append(down)
        line = jnp.stack(below + [rows] + above)
        line = lax.dynamic_slice_in_dim(line, chips - 1 - z, chips, 0)
        picked = jnp.einsum(
            "nct,ntd->ncd", fwd_own, line, preferred_element_type=jnp.float32
        ).astype(jnp.bfloat16)
        picked_other = partner_of(picked)
        projected_own += jnp.einsum(
            "ncd,dh->nch", picked, own_weights, preferred_element_type=jnp.float32
        )
        projected_other += jnp.einsum(
            "ncd,dh->nch", picked_other, own_weights, preferred_element_type=jnp.float32
        )

        partial_other = jnp.einsum(
            "nch,dh->ncd", grad_other, own_weights, preferred_element_type=jnp.float32
        ).astype(jnp.bfloat16)
        received = partner_of(partial_other)
        partial_own = jnp.einsum(
            "nch,dh->ncd", grad_own, own_weights, preferred_element_type=jnp.float32
        ).astype(jnp.bfloat16)
        pair = (partial_own.astype(jnp.float32) + received.astype(jnp.float32)).astype(
            jnp.bfloat16
        )
        terms = jnp.einsum(
            "nct,ncd->ntd", bwd_own, pair, preferred_element_type=jnp.float32
        ).astype(jnp.bfloat16)
        up = down = 0.0
        for hop in range(1, chips):
            above_term = lax.dynamic_index_in_dim(
                terms, jnp.minimum(z + chips - hop, chips - 1), 0, keepdims=False
            )
            below_term = lax.dynamic_index_in_dim(
                terms, jnp.maximum(z - chips + hop, 0), 0, keepdims=False
            )
            up = step_along((above_term + up).astype(jnp.bfloat16), 0, hop - 1, 1)
            down = step_along((below_term + down).astype(jnp.bfloat16), chips - hop, chips - 1, -1)
        mine = lax.dynamic_index_in_dim(terms, z, 0, keepdims=False)
        grad_in = (
            mine.astype(jnp.float32) + up.astype(jnp.float32) + down.astype(jnp.float32)
        ).astype(jnp.bfloat16)
        grad_rows.append(shifted(grad_in, "pp", -1))

    def activated(projected):
        return (jax.nn.silu(projected[..., :hid_units]) * projected[..., hid_units:]).astype(
            jnp.bfloat16
        )

    own, other = activated(projected_own), activated(projected_other)
    hidden = jnp.stack(
        [jnp.where(core == 0, own, other), jnp.where(core == 0, other, own)], axis=1
    ).reshape(groups, capacity, hid_units)
    return hidden[None, None], jnp.concatenate(grad_rows, axis=1)[None]


def solution(mesh):
    placed = (
        P("pp", "ep", None),
        P("pp", "ep", None),
        P("pp", "ep", None, None),
        P("pp", "ep", None),
        P("pp", "ep", None, None, None),
        P("pp", "ep", None, None, None),
    )
    return jax.shard_map(
        shards,
        mesh=mesh,
        in_specs=placed,
        out_specs=(P("pp", "ep", None, None, None), P("pp", "ep", None)),
        check_vma=False,
    )
```

time: 354 us -> 333 us (0.941)
  waiting for transfers between devices: 254 us -> 133 us
  starting transfers between devices: 15.3 us -> 88.8 us
  blocking collectives: 0 us -> 26.8 us
  other arithmetic: 31.2 us -> 10.9 us
  matrix products: 42.6 us -> 55 us
  local copies, waits for them, and re-layouts: 9.71 us -> 16 us
    all_to_all x2 -> x0, waiting for transfers between devices: 200 us -> none  [the longest x1 118 us: shards(): lax.all_to_all(pair_half, 'ep', split_axis=0, concat_axis=0, tiled=True)]
    ppermute x2 -> x28, waiting for transfers between devices: 8.87 us -> 92.5 us  [the longest x24 92.5 us: step_along(): return lax.ppermute(value, 'ep', pairs)]
    ppermute x2 -> x28, starting transfers between devices: 0.71 us -> 81.3 us  [the longest x24 80.4 us: step_along(): return lax.ppermute(value, 'ep', pairs)]
    all_gather x0 -> x1, blocking collectives: none -> 26.8 us  [shards(): lax.all_gather(jnp.concatenate([fwd_experts[0], bwd_experts[0]], axis=1),...]
    select_n x2, other arithmetic: 16.7 us -> 0.01 us  [slots_of(): place = jnp.where(named == 1, slot, -1)]
    dot_general x4 -> x10, matrix products: 42.6 us -> 55 us  [the longest x2 19.7 us: shards(): jnp.einsum('nct,ncd->ntd', bwd_own, pair, preferred_element_type=jnp.floa...]
    all_to_all x2 -> x0, starting transfers between devices: 10.1 us -> none  [the longest x1 5.2 us: shards(): lax.all_to_all(outgoing, 'ep', split_axis=0, concat_axis=0, tiled=True)]
    unnamed x15 -> x41, local copies, waits for them, and re-layouts: 2.38 us -> 10.3 us
  transfers between devices with their start and end apart: 6 -> 32, of which waited for: 5 -> 10; matrix products, arithmetic and copies ran while one was open for 22% -> 21% of each run, Pallas kernels for 0% -> 0%
where the time goes in v1:
time: 333 us; the launch traced here: 332 us
  waiting for transfers between devices  133 us (40%)
  starting transfers between devices  88.8 us (27%)
  matrix products  55 us (17%)
  blocking collectives  26.8 us (8%)
  local copies, waits for them, and re-layouts  16 us (5%)
  other arithmetic  10.9 us (3%)
    ppermute x24, waiting for transfers between devices, step_along(): return lax.ppermute(value, 'ep', pairs)  92.5 us
    ppermute x24, starting transfers between devices, step_along(): return lax.ppermute(value, 'ep', pairs)  80.4 us
    ppermute x4, waiting for transfers between devices, shifted(): return lax.ppermute(block, axis, route)  40.4 us
    all_gather x1, blocking collectives, shards(): lax.all_gather(jnp.concatenate([fwd_experts[0], bwd_experts[0]], axis=1),...  26.8 us
    dot_general x2, matrix products, shards(): jnp.einsum('nct,ncd->ntd', bwd_own, pair, preferred_element_type=jnp.floa...  19.7 us
    dot_general x2, matrix products, shards(): jnp.einsum('nch,dh->ncd', grad_other, own_weights, preferred_element_type...  12.9 us
    dot_general x2, matrix products, shards(): jnp.einsum('ncd,dh->nch', picked, own_weights, preferred_element_type=jnp...  10.8 us
    unnamed x41, local copies, waits for them, and re-layouts  10.3 us
  transfers between devices with their start and end apart: 32, of which 10 were waited for; matrix products, arithmetic and copies ran while one was open for 21% of the time, Pallas kernels for 0%

profile of v1, /device:TPU:0, one launch (start us, length us, event | category | flops | bytes accessed | tf_op | source)
XLA Modules:
  0.0 331.8 jit_solution(14972895991798406873)
XLA Ops:
  0.6 1.8 bitcast_convert_fusion
  2.5 1.9 fusion.60
  4.4 8.4 %fusion.31 = bf16[4,96,3584]{2,1,0:T(8,128)(2,1)} fusion(bf16[1,1,7168,1024]{3,2,1,0:T(8,128)(2,1)} %param.8, s32[]{:T(128)S(6)} %select_n.84, bf16[4,2,96,512]{3,2,1,0:T(8,128)(2,1)S(1)} %bitcast.161, bf16[4,2,96,512]{3,2,1,0:T(8,128)(2,1)S(1)} %bitcast.157), kind=kOutput, calls=%fused_computation.25 | convolution fusion | flops 2821521408 | bytes 11665412 | tf_op jit(solution)/shard_map/nch,dh->ncd/dot_general | solution.py:103
  13.3 2.5 collective-permute-start.7
  15.9 1.5 collective-permute-start
  17.4 20.8 %collective-permute-done.7 = bf16[128,3584]{1,0:T(8,128)(2,1)} collective-permute-done((bf16[128,3584]{1,0:T(8,128)(2,1)S(1)}, bf16[128,3584]{1,0:T(8,128)(2,1)}, u32[]{:S(2)}, u32[]{:S(2)}) %collective-permute-start.7) | collective-permute-done | bytes 917536 | tf_op jit(solution)/shard_map/ppermute | solution.py:12
  38.1 4.8 %collective-permute-start.8 = (bf16[128,3584]{1,0:T(8,128)(2,1)}, bf16[128,3584]{1,0:T(8,128)(2,1)}, u32[]{:S(2)}, u32[]{:S(2)}) collective-permute-start(bf16[128,3584]{1,0:T(8,128)(2,1)} %collective-permute-done.7), channel_id=1, source_target_pairs={{0,2},{1,3},{2,4},{3,5},{4,6},{5,7},{8,10},{9,11},{10,12},{11,13},... | collective-permute-start | bytes 2752520 | tf_op jit(solution)/shard_map/ppermute | solution.py:22
  42.9 1.3 collective-permute-start.11
  44.2 13.3 %collective-permute-done = bf16[128,3584]{1,0:T(8,128)(2,1)S(1)} collective-permute-done((bf16[128,3584]{1,0:T(8,128)(2,1)S(1)}, bf16[128,3584]{1,0:T(8,128)(2,1)S(1)}, u32[]{:S(2)}, u32[]{:S(2)}) %collective-permute-start) | collective-permute-done | bytes 917536 | tf_op jit(solution)/shard_map/ppermute | solution.py:12
  57.5 3.7 %collective-permute-start.1 = (bf16[128,3584]{1,0:T(8,128)(2,1)S(1)}, bf16[128,3584]{1,0:T(8,128)(2,1)S(1)}, u32[]{:S(2)}, u32[]{:S(2)}) collective-permute-start(bf16[128,3584]{1,0:T(8,128)(2,1)S(1)} %collective-permute-done), channel_id=1, source_target_pairs={{0,2},{1,3},{2,4},{3,5},{4,6},{5,7},{8,10},{9,11},{10,12},{11,13},... | collective-permute-start | bytes 2752520 | tf_op jit(solution)/shard_map/ppermute | solution.py:22
  61.2 1.3 collective-permute-start.4
  62.6 4.5 %fusion.22 = bf16[4,96,3584]{2,1,0:T(8,128)(2,1)} fusion(bf16[1,1,7168,1024]{3,2,1,0:T(8,128)(2,1)S(1)} %copy-done.9, s32[]{:T(128)S(6)} %select_n.84, bf16[4,2,96,512]{3,2,1,0:T(8,128)(2,1)S(1)} %bitcast.162, bf16[4,2,96,512]{3,2,1,0:T(8,128)(2,1)S(1)} %bitcast.158), kind=kOutput, calls=%fused_computation.22 | convolution fusion | flops 2821521408 | bytes 11665412 | tf_op jit(solution)/shard_map/nch,dh->ncd/dot_general | solution.py:103
  67.1 26.8 %all-gather = s32[1024,4]{0,1:T(4,128)S(1)} all-gather(s32[128,4]{0,1:T(4,128)S(1)} %pad_add_fusion), channel_id=2, replica_groups=mesh['pp'=4,'ep'=8] {'ep'}, dimensions={0}, use_global_device_ids=true | all-gather | bytes 18432 | tf_op jit(solution)/shard_map/all_gather | solution.py:58
  96.5 1.6 collective-permute-start.9
  98.1 1.3 collective-permute-start.12
  99.4 1.6 collective-permute-start.2
  101.0 1.3 collective-permute-start.5
  102.3 9.9 %convolution_convert_fusion = bf16[4,128,3584]{2,1,0:T(8,128)(2,1)} fusion(bf16[4,96,3584]{2,1,0:T(8,128)(2,1)} %collective-permute-done.24, bf16[1,1,7168,1024]{3,2,1,0:T(8,128)(2,1)} %param.8, s32[4,1,128]{2,0,1:T(4,128)S(1)} %constant_dynamic-slice_fusion, s32[]{:T(128)S(6)} %select_n.79, bf16[4,2,96,512]{3,2,1,0:T(8,128)(2,1)} %bitcast.163, ...), kind=kOutput, calls=%fused_computation.16 | convolution fusion | flops 3181232128 | bytes 15337476 | tf_op jit(solution)/shard_map/nct,ncd->ntd/dot_general | solution.py:113
  112.2 2.9 dynamic-slice_bitcast_fusion.1
  115.1 11.0 %collective-permute-start.25 = (bf16[128,3584]{1,0:T(8,128)(2,1)}, bf16[128,3584]{1,0:T(8,128)(2,1)}, u32[]{:S(2)}, u32[]{:S(2)}) collective-permute-start(bf16[128,3584]{1,0:T(8,128)(2,1)} %get-tuple-element.15), channel_id=1, source_target_pairs={{0,2},{1,3},{8,10},{9,11},{16,18},{17,19},{24,26},{25,27}} | collective-permute-start | bytes 2752520 | tf_op jit(solution)/shard_map/ppermute | solution.py:22
  126.1 1.6 collective-permute-start.10
  127.7 9.8 %convolution_convert_fusion.1 = bf16[4,128,3584]{2,1,0:T(8,128)(2,1)} fusion(bf16[4,96,3584]{2,1,0:T(8,128)(2,1)} %collective-permute-done.16, bf16[1,1,7168,1024]{3,2,1,0:T(8,128)(2,1)} %param.8, s32[4,1,128]{2,0,1:T(4,128)S(1)} %constant_dynamic-slice_fusion, s32[]{:T(128)S(6)} %select_n.79, bf16[4,2,96,512]{3,2,1,0:T(8,128)(2,1)} %bitcast.164, ...), kind=kOutput, calls=%fused_computation.17 | convolution fusion | flops 3181232128 | bytes 15337476 | tf_op jit(solution)/shard_map/nct,ncd->ntd/dot_general | solution.py:113
  137.5 1.7 dynamic-slice_bitcast_fusion.3
  140.0 1.3 collective-permute-start.13
  148.8 4.7 %collective-permute-start.17 = (bf16[128,3584]{1,0:T(8,128)(2,1)S(1)}, bf16[128,3584]{1,0:T(8,128)(2,1)S(1)}, u32[]{:S(2)}, u32[]{:S(2)}) collective-permute-start(bf16[128,3584]{1,0:T(8,128)(2,1)S(1)} %get-tuple-element.11), channel_id=1, source_target_pairs={{0,2},{1,3},{8,10},{9,11},{16,18},{17,19},{24,26},{25,27}} | collective-permute-start | bytes 2752520 | tf_op jit(solution)/shard_map/ppermute | solution.py:22
  153.4 10.1 %collective-permute-done.13 = bf16[128,3584]{1,0:T(8,128)(2,1)S(1)} collective-permute-done((bf16[128,3584]{1,0:T(8,128)(2,1)}, bf16[128,3584]{1,0:T(8,128)(2,1)S(1)}, u32[]{:S(2)}, u32[]{:S(2)}) %collective-permute-start.13) | collective-permute-done | bytes 917536 | tf_op jit(solution)/shard_map/ppermute | solution.py:22
  165.9 1.3 collective-permute-start.6
  170.0 18.6 %collective-permute-done.6 = bf16[128,3584]{1,0:T(8,128)(2,1)S(1)} collective-permute-done((bf16[128,3584]{1,0:T(8,128)(2,1)}, bf16[128,3584]{1,0:T(8,128)(2,1)S(1)}, u32[]{:S(2)}, u32[]{:S(2)}) %collective-permute-start.6) | collective-permute-done | bytes 917536 | tf_op jit(solution)/shard_map/ppermute | solution.py:22
  189.6 5.4 %fusion.6 = f32[4,96,1024]{2,1,0:T(8,128)S(1)} fusion(bf16[4,96,3584]{2,1,0:T(8,128)(2,1)S(1)} %convolution_convert_fusion.2, bf16[1,1,7168,1024]{3,2,1,0:T(8,128)(2,1)} %param.8), kind=kOutput, calls=%fused_computation.6 | convolution fusion | flops 2818572288 | bytes 11665408 | tf_op jit(solution)/shard_map/ncd,dh->nch/dot_general | solution.py:96
  195.4 1.3 bitcast_add_fusion.2
  196.8 1.6 collective-permute-start.26
  198.5 5.4 %fusion.61 = f32[4,96,1024]{2,1,0:T(8,128)S(1)} fusion(f32[4,96,1024]{2,1,0:T(8,128)S(1)} %fusion.6, bf16[4,96,3584]{2,1,0:T(8,128)(2,1)S(1)} %convolution_convert_fusion.3, bf16[1,1,7168,1024]{3,2,1,0:T(8,128)(2,1)} %param.8), kind=kOutput, calls=%fused_computation.58 | convolution fusion | flops 2818965504 | bytes 13238272 | tf_op jit(solution)/shard_map/ncd,dh->nch/dot_general | solution.py:96
  204.0 10.7 %collective-permute-start.18 = (bf16[128,3584]{1,0:T(8,128)(2,1)S(1)}, bf16[128,3584]{1,0:T(8,128)(2,1)S(1)}, u32[]{:S(2)}, u32[]{:S(2)}) collective-permute-start(bf16[128,3584]{1,0:T(8,128)(2,1)S(1)} %bitcast_add_fusion.6), channel_id=1, source_target_pairs={{0,2},{1,3},{2,4},{3,5},{8,10},{9,11},{10,12},{11,13},{16,18},{17,... | collective-permute-start | bytes 2752520 | tf_op jit(solution)/shard_map/ppermute | solution.py:22
  214.7 4.3 %collective-permute-done.26 = bf16[128,3584]{1,0:T(8,128)(2,1)S(1)} collective-permute-done((bf16[128,3584]{1,0:T(8,128)(2,1)S(1)}, bf16[128,3584]{1,0:T(8,128)(2,1)S(1)}, u32[]{:S(2)}, u32[]{:S(2)}) %collective-permute-start.26) | collective-permute-done | bytes 917536 | tf_op jit(solution)/shard_map/ppermute | solution.py:22
  220.0 11.6 %collective-permute-start.27 = (bf16[128,3584]{1,0:T(8,128)(2,1)S(1)}, bf16[128,3584]{1,0:T(8,128)(2,1)S(1)}, u32[]{:S(2)}, u32[]{:S(2)}) collective-permute-start(bf16[128,3584]{1,0:T(8,128)(2,1)S(1)} %get-tuple-element.13), channel_id=1, source_target_pairs={{0,2},{1,3},{2,4},{3,5},{4,6},{5,7},{8,10},{9,11},{10,12},{11,13},... | collective-permute-start | bytes 2752520 | tf_op jit(solution)/shard_map/ppermute | solution.py:22
  231.6 7.1 %collective-permute-done.18 = bf16[128,3584]{1,0:T(8,128)(2,1)S(1)} collective-permute-done((bf16[128,3584]{1,0:T(8,128)(2,1)S(1)}, bf16[128,3584]{1,0:T(8,128)(2,1)S(1)}, u32[]{:S(2)}, u32[]{:S(2)}) %collective-permute-start.18) | collective-permute-done | bytes 917536 | tf_op jit(solution)/shard_map/ppermute | solution.py:22
  239.6 13.5 %collective-permute-start.19 = (bf16[128,3584]{1,0:T(8,128)(2,1)S(1)}, bf16[128,3584]{1,0:T(8,128)(2,1)S(1)}, u32[]{:S(2)}, u32[]{:S(2)}) collective-permute-start(bf16[128,3584]{1,0:T(8,128)(2,1)S(1)} %get-tuple-element.9), channel_id=1, source_target_pairs={{0,2},{1,3},{2,4},{3,5},{4,6},{5,7},{8,10},{9,11},{10,12},{11,13},... | collective-permute-start | bytes 2752520 | tf_op jit(solution)/shard_map/ppermute | solution.py:22
  253.3 1.3 collective-permute-start.30
  254.7 3.6 %collective-permute-done.27 = bf16[128,3584]{1,0:T(8,128)(2,1)S(1)} collective-permute-done((bf16[128,3584]{1,0:T(8,128)(2,1)S(1)}, bf16[128,3584]{1,0:T(8,128)(2,1)S(1)}, u32[]{:S(2)}, u32[]{:S(2)}) %collective-permute-start.27) | collective-permute-done | bytes 917536 | tf_op jit(solution)/shard_map/ppermute | solution.py:22
  258.3 1.3 collective-permute-start.22
  259.6 34.4 %collective-permute-done.30 = bf16[128,3584]{1,0:T(8,128)(2,1)S(1)} collective-permute-done((bf16[128,3584]{1,0:T(8,128)(2,1)S(1)}, bf16[128,3584]{1,0:T(8,128)(2,1)S(1)}, u32[]{:S(2)}, u32[]{:S(2)}) %collective-permute-start.30) | collective-permute-done | bytes 917536 | tf_op jit(solution)/shard_map/ppermute | solution.py:22
  294.4 1.8 collective-permute-start.31
  296.2 14.4 %collective-permute-done.22 = bf16[128,3584]{1,0:T(8,128)(2,1)S(1)} collective-permute-done((bf16[128,3584]{1,0:T(8,128)(2,1)S(1)}, bf16[128,3584]{1,0:T(8,128)(2,1)S(1)}, u32[]{:S(2)}, u32[]{:S(2)}) %collective-permute-start.22) | collective-permute-done | bytes 917536 | tf_op jit(solution)/shard_map/ppermute | solution.py:22
  310.9 1.6 collective-permute-start.23
  312.5 4.9 %fusion.4 = f32[4,96,1024]{2,1,0:T(8,128)S(1)} fusion(bf16[4,96,3584]{2,1,0:T(8,128)(2,1)} %collective-permute-done.15, bf16[1,1,7168,1024]{3,2,1,0:T(8,128)(2,1)S(1)} %bitcast.174), kind=kOutput, calls=%fused_computation.4 | convolution fusion | flops 2818572288 | bytes 11665408 | tf_op jit(solution)/shard_map/ncd,dh->nch/dot_general | solution.py:99
  317.5 4.9 %fusion.64 = f32[4,96,1024]{2,1,0:T(8,128)S(1)} fusion(f32[4,96,1024]{2,1,0:T(8,128)S(1)} %fusion.4, bf16[4,96,3584]{2,1,0:T(8,128)(2,1)} %collective-permute-done.14, bf16[1,1,7168,1024]{3,2,1,0:T(8,128)(2,1)S(1)} %bitcast.174), kind=kOutput, calls=%fused_computation.59 | convolution fusion | flops 2818965504 | bytes 13238272 | tf_op jit(solution)/shard_map/ncd,dh->nch/dot_general | solution.py:99
  324.0 6.4 %collective-permute-done.23 = bf16[128,3584]{1,0:T(8,128)(2,1)S(1)} collective-permute-done((bf16[128,3584]{1,0:T(8,128)(2,1)S(1)}, bf16[128,3584]{1,0:T(8,128)(2,1)S(1)}, u32[]{:S(2)}, u32[]{:S(2)}) %collective-permute-start.23) | collective-permute-done | bytes 917536 | tf_op jit(solution)/shard_map/ppermute | solution.py:12
  330.4 1.4 maximum_bitcast_fusion
  (101 shorter events, 22.3 us)
Async XLA Ops:
  4.3 58.2 %copy-start.4 = (bf16[8,96,512]{2,1,0:T(8,128)(2,1)}, bf16[8,96,512]{2,1,0:T(8,128)(2,1)S(1)}, u32[]{:S(2)}) copy-start(bf16[8,96,512]{2,1,0:T(8,128)(2,1)S(1)} %get-tuple-element.7) | copy-start | bytes 2359300
  4.3 58.2 %copy-start.6 = (bf16[8,96,512]{2,1,0:T(8,128)(2,1)}, bf16[8,96,512]{2,1,0:T(8,128)(2,1)S(1)}, u32[]{:S(2)}) copy-start(bf16[8,96,512]{2,1,0:T(8,128)(2,1)S(1)} %get-tuple-element.8) | copy-start | bytes 2359300
  4.3 8.9 %copy-start.2 = (bf16[1,128,7168]{2,1,0:T(8,128)(2,1)S(1)}, bf16[1,128,7168]{2,1,0:T(8,128)(2,1)}, u32[]{:S(2)}) copy-start(bf16[1,128,7168]{2,1,0:T(8,128)(2,1)} %param.6) | copy-start | bytes 5505028
  4.4 58.2 %copy-start.9 = (bf16[1,1,7168,1024]{3,2,1,0:T(8,128)(2,1)S(1)}, bf16[1,1,7168,1024]{3,2,1,0:T(8,128)(2,1)}, u32[]{:S(2)}) copy-start(bf16[1,1,7168,1024]{3,2,1,0:T(8,128)(2,1)} %param.8) | copy-start | bytes 44040196
  12.7 88.3 %collective-permute-start.24 = (bf16[4,96,3584]{2,1,0:T(8,128)(2,1)}, bf16[4,96,3584]{2,1,0:T(8,128)(2,1)}, u32[]{:S(2)}, u32[]{:S(2)}) collective-permute-start(bf16[4,96,3584]{2,1,0:T(8,128)(2,1)} %fusion.31), channel_id=1, source_target_pairs={{0,1},{1,0},{2,3},{3,2},{4,5},{5,4},{6,7},{7,6},{8,9},{9,8},{10,11... | collective-permute-start | bytes 8257544 | tf_op jit(solution)/shard_map/ppermute | solution.py:17
  13.3 24.8 %collective-permute-start.7 = (bf16[128,3584]{1,0:T(8,128)(2,1)S(1)}, bf16[128,3584]{1,0:T(8,128)(2,1)}, u32[]{:S(2)}, u32[]{:S(2)}) collective-permute-start(bf16[128,3584]{1,0:T(8,128)(2,1)S(1)} %get-tuple-element.18), channel_id=1, source_target_pairs={{24,0},{0,8},{8,16},{16,24},{25,1},{1,9},{9,17},{17,25},{26,2},{2,... | collective-permute-start | bytes 2752520 | tf_op jit(solution)/shard_map/ppermute | solution.py:12
  15.9 51.2 %copy-start.7 = (s32[1,128,2]{1,2,0:T(2,128)S(1)}, s32[1,128,2]{1,2,0:T(2,128)}, u32[]{:S(2)}) copy-start(s32[1,128,2]{1,2,0:T(2,128)} %param.9) | copy-start | bytes 3076
  15.9 51.2 %copy-start.8 = (s32[1,128,2]{1,2,0:T(2,128)S(1)}, s32[1,128,2]{1,2,0:T(2,128)}, u32[]{:S(2)}) copy-start(s32[1,128,2]{1,2,0:T(2,128)} %param.7) | copy-start | bytes 3076
  15.9 41.6 %collective-permute-start = (bf16[128,3584]{1,0:T(8,128)(2,1)S(1)}, bf16[128,3584]{1,0:T(8,128)(2,1)S(1)}, u32[]{:S(2)}, u32[]{:S(2)}) collective-permute-start(bf16[128,3584]{1,0:T(8,128)(2,1)S(1)} %get-tuple-element.17), channel_id=1, source_target_pairs={{24,0},{0,8},{8,16},{16,24},{25,1},{1,9},{9,17},{17,25},{26,2},{2,... | collective-permute-start | bytes 2752520 | tf_op jit(solution)/shard_map/ppermute | solution.py:12
  38.1 28.9 %collective-permute-start.8 = (bf16[128,3584]{1,0:T(8,128)(2,1)}, bf16[128,3584]{1,0:T(8,128)(2,1)}, u32[]{:S(2)}, u32[]{:S(2)}) collective-permute-start(bf16[128,3584]{1,0:T(8,128)(2,1)} %collective-permute-done.7), channel_id=1, source_target_pairs={{0,2},{1,3},{2,4},{3,5},{4,6},{5,7},{8,10},{9,11},{10,12},{11,13},... | collective-permute-start | bytes 2752520 | tf_op jit(solution)/shard_map/ppermute | solution.py:22
  42.9 53.5 %collective-permute-start.11 = (bf16[128,3584]{1,0:T(8,128)(2,1)}, bf16[128,3584]{1,0:T(8,128)(2,1)}, u32[]{:S(2)}, u32[]{:S(2)}) collective-permute-start(bf16[128,3584]{1,0:T(8,128)(2,1)} %collective-permute-done.7), channel_id=1, source_target_pairs={{2,0},{3,1},{4,2},{5,3},{6,4},{7,5},{10,8},{11,9},{12,10},{13,11},... | collective-permute-start | bytes 2752520 | tf_op jit(solution)/shard_map/ppermute | solution.py:22
  57.5 40.6 %collective-permute-start.1 = (bf16[128,3584]{1,0:T(8,128)(2,1)S(1)}, bf16[128,3584]{1,0:T(8,128)(2,1)S(1)}, u32[]{:S(2)}, u32[]{:S(2)}) collective-permute-start(bf16[128,3584]{1,0:T(8,128)(2,1)S(1)} %collective-permute-done), channel_id=1, source_target_pairs={{0,2},{1,3},{2,4},{3,5},{4,6},{5,7},{8,10},{9,11},{10,12},{11,13},... | collective-permute-start | bytes 2752520 | tf_op jit(solution)/shard_map/ppermute | solution.py:22
  61.2 38.1 %collective-permute-start.4 = (bf16[128,3584]{1,0:T(8,128)(2,1)S(1)}, bf16[128,3584]{1,0:T(8,128)(2,1)S(1)}, u32[]{:S(2)}, u32[]{:S(2)}) collective-permute-start(bf16[128,3584]{1,0:T(8,128)(2,1)S(1)} %collective-permute-done), channel_id=1, source_target_pairs={{2,0},{3,1},{4,2},{5,3},{6,4},{7,5},{10,8},{11,9},{12,10},{13,11},... | collective-permute-start | bytes 2752520 | tf_op jit(solution)/shard_map/ppermute | solution.py:22
  67.1 59.1 %collective-permute-start.16 = (bf16[4,96,3584]{2,1,0:T(8,128)(2,1)}, bf16[4,96,3584]{2,1,0:T(8,128)(2,1)}, u32[]{:S(2)}, u32[]{:S(2)}) collective-permute-start(bf16[4,96,3584]{2,1,0:T(8,128)(2,1)} %fusion.22), channel_id=1, source_target_pairs={{0,1},{1,0},{2,3},{3,2},{4,5},{5,4},{6,7},{7,6},{8,9},{9,8},{10,11... | collective-permute-start | bytes 8257544 | tf_op jit(solution)/shard_map/ppermute | solution.py:17
  96.5 18.6 %collective-permute-start.9 = (bf16[128,3584]{1,0:T(8,128)(2,1)}, bf16[128,3584]{1,0:T(8,128)(2,1)}, u32[]{:S(2)}, u32[]{:S(2)}) collective-permute-start(bf16[128,3584]{1,0:T(8,128)(2,1)} %collective-permute-done.8), channel_id=1, source_target_pairs={{2,4},{3,5},{4,6},{5,7},{10,12},{11,13},{12,14},{13,15},{18,20},{1... | collective-permute-start | bytes 2752520 | tf_op jit(solution)/shard_map/ppermute | solution.py:22
  98.1 41.1 %collective-permute-start.12 = (bf16[128,3584]{1,0:T(8,128)(2,1)}, bf16[128,3584]{1,0:T(8,128)(2,1)}, u32[]{:S(2)}, u32[]{:S(2)}) collective-permute-start(bf16[128,3584]{1,0:T(8,128)(2,1)} %collective-permute-done.11), channel_id=1, source_target_pairs={{2,0},{3,1},{4,2},{5,3},{10,8},{11,9},{12,10},{13,11},{18,16},{19,... | collective-permute-start | bytes 2752520 | tf_op jit(solution)/shard_map/ppermute | solution.py:22
  99.4 49.4 %collective-permute-start.2 = (bf16[128,3584]{1,0:T(8,128)(2,1)S(1)}, bf16[128,3584]{1,0:T(8,128)(2,1)}, u32[]{:S(2)}, u32[]{:S(2)}) collective-permute-start(bf16[128,3584]{1,0:T(8,128)(2,1)S(1)} %collective-permute-done.1), channel_id=1, source_target_pairs={{2,4},{3,5},{4,6},{5,7},{10,12},{11,13},{12,14},{13,15},{18,20},{1... | collective-permute-start | bytes 2752520 | tf_op jit(solution)/shard_map/ppermute | solution.py:22
  101.0 64.2 %collective-permute-start.5 = (bf16[128,3584]{1,0:T(8,128)(2,1)S(1)}, bf16[128,3584]{1,0:T(8,128)(2,1)}, u32[]{:S(2)}, u32[]{:S(2)}) collective-permute-start(bf16[128,3584]{1,0:T(8,128)(2,1)S(1)} %collective-permute-done.4), channel_id=1, source_target_pairs={{2,0},{3,1},{4,2},{5,3},{10,8},{11,9},{12,10},{13,11},{18,16},{19,... | collective-permute-start | bytes 2752520 | tf_op jit(solution)/shard_map/ppermute | solution.py:22
  112.2 15.5 %copy-start.5 = (bf16[8,96,512]{2,1,0:T(8,128)(2,1)S(1)}, bf16[8,96,512]{2,1,0:T(8,128)(2,1)}, u32[]{:S(2)}) copy-start(bf16[8,96,512]{2,1,0:T(8,128)(2,1)} %copy-done.4) | copy-start | bytes 2359300
  115.1 79.9 %collective-permute-start.25 = (bf16[128,3584]{1,0:T(8,128)(2,1)}, bf16[128,3584]{1,0:T(8,128)(2,1)}, u32[]{:S(2)}, u32[]{:S(2)}) collective-permute-start(bf16[128,3584]{1,0:T(8,128)(2,1)} %get-tuple-element.15), channel_id=1, source_target_pairs={{0,2},{1,3},{8,10},{9,11},{16,18},{17,19},{24,26},{25,27}} | collective-permute-start | bytes 2752520 | tf_op jit(solution)/shard_map/ppermute | solution.py:22
  126.1 13.9 %collective-permute-start.10 = (bf16[128,3584]{1,0:T(8,128)(2,1)}, bf16[128,3584]{1,0:T(8,128)(2,1)}, u32[]{:S(2)}, u32[]{:S(2)}) collective-permute-start(bf16[128,3584]{1,0:T(8,128)(2,1)} %collective-permute-done.9), channel_id=1, source_target_pairs={{4,6},{5,7},{12,14},{13,15},{20,22},{21,23},{28,30},{29,31}} | collective-permute-start | bytes 2752520 | tf_op jit(solution)/shard_map/ppermute | solution.py:22
  137.5 1.7 copy-start.3
  139.3 64.7 %collective-permute-start.28 = (bf16[128,3584]{1,0:T(8,128)(2,1)S(1)}, bf16[128,3584]{1,0:T(8,128)(2,1)S(1)}, u32[]{:S(2)}, u32[]{:S(2)}) collective-permute-start(bf16[128,3584]{1,0:T(8,128)(2,1)S(1)} %copy-done.3), channel_id=1, source_target_pairs={{6,4},{7,5},{14,12},{15,13},{22,20},{23,21},{30,28},{31,29}} | collective-permute-start | bytes 2752520 | tf_op jit(solution)/shard_map/ppermute | solution.py:22
  140.0 23.5 %collective-permute-start.13 = (bf16[128,3584]{1,0:T(8,128)(2,1)}, bf16[128,3584]{1,0:T(8,128)(2,1)S(1)}, u32[]{:S(2)}, u32[]{:S(2)}) collective-permute-start(bf16[128,3584]{1,0:T(8,128)(2,1)} %collective-permute-done.12), channel_id=1, source_target_pairs={{2,0},{3,1},{10,8},{11,9},{18,16},{19,17},{26,24},{27,25}} | collective-permute-start | bytes 2752520 | tf_op jit(solution)/shard_map/ppermute | solution.py:22
  148.8 48.0 %collective-permute-start.17 = (bf16[128,3584]{1,0:T(8,128)(2,1)S(1)}, bf16[128,3584]{1,0:T(8,128)(2,1)S(1)}, u32[]{:S(2)}, u32[]{:S(2)}) collective-permute-start(bf16[128,3584]{1,0:T(8,128)(2,1)S(1)} %get-tuple-element.11), channel_id=1, source_target_pairs={{0,2},{1,3},{8,10},{9,11},{16,18},{17,19},{24,26},{25,27}} | collective-permute-start | bytes 2752520 | tf_op jit(solution)/shard_map/ppermute | solution.py:22
  163.5 2.4 collective-permute-start.3
  165.2 54.7 %collective-permute-start.20 = (bf16[128,3584]{1,0:T(8,128)(2,1)S(1)}, bf16[128,3584]{1,0:T(8,128)(2,1)S(1)}, u32[]{:S(2)}, u32[]{:S(2)}) collective-permute-start(bf16[128,3584]{1,0:T(8,128)(2,1)S(1)} %get-tuple-element.12), channel_id=1, source_target_pairs={{6,4},{7,5},{14,12},{15,13},{22,20},{23,21},{30,28},{31,29}} | collective-permute-start | bytes 2752520 | tf_op jit(solution)/shard_map/ppermute | solution.py:22
  165.9 22.6 %collective-permute-start.6 = (bf16[128,3584]{1,0:T(8,128)(2,1)}, bf16[128,3584]{1,0:T(8,128)(2,1)S(1)}, u32[]{:S(2)}, u32[]{:S(2)}) collective-permute-start(bf16[128,3584]{1,0:T(8,128)(2,1)} %collective-permute-done.5), channel_id=1, source_target_pairs={{2,0},{3,1},{10,8},{11,9},{18,16},{19,17},{26,24},{27,25}} | collective-permute-start | bytes 2752520 | tf_op jit(solution)/shard_map/ppermute | solution.py:22
  189.5 5.9 %copy-start = (bf16[4,128,3584]{2,1,0:T(8,128)(2,1)S(1)}, bf16[4,128,3584]{2,1,0:T(8,128)(2,1)}, u32[]{:S(2)}) copy-start(bf16[4,128,3584]{2,1,0:T(8,128)(2,1)} %convolution_convert_fusion) | copy-start | bytes 11010052
  189.5 8.9 %copy-start.1 = (bf16[4,128,3584]{2,1,0:T(8,128)(2,1)S(1)}, bf16[4,128,3584]{2,1,0:T(8,128)(2,1)}, u32[]{:S(2)}) copy-start(bf16[4,128,3584]{2,1,0:T(8,128)(2,1)} %convolution_convert_fusion.1) | copy-start | bytes 11010052
  189.5 123.0 %collective-permute-start.15 = (bf16[4,96,3584]{2,1,0:T(8,128)(2,1)S(1)}, bf16[4,96,3584]{2,1,0:T(8,128)(2,1)}, u32[]{:S(2)}, u32[]{:S(2)}) collective-permute-start(bf16[4,96,3584]{2,1,0:T(8,128)(2,1)S(1)} %convolution_convert_fusion.2), channel_id=1, source_target_pairs={{0,1},{1,0},{2,3},{3,2},{4,5},{5,4},{6,7},{7,6},{8,9},{9,8},{10,11... | collective-permute-start | bytes 8257544 | tf_op jit(solution)/shard_map/ppermute | solution.py:17
  195.0 122.4 %collective-permute-start.14 = (bf16[4,96,3584]{2,1,0:T(8,128)(2,1)S(1)}, bf16[4,96,3584]{2,1,0:T(8,128)(2,1)}, u32[]{:S(2)}, u32[]{:S(2)}) collective-permute-start(bf16[4,96,3584]{2,1,0:T(8,128)(2,1)S(1)} %convolution_convert_fusion.3), channel_id=1, source_target_pairs={{0,1},{1,0},{2,3},{3,2},{4,5},{5,4},{6,7},{7,6},{8,9},{9,8},{10,11... | collective-permute-start | bytes 8257544 | tf_op jit(solution)/shard_map/ppermute | solution.py:17
  196.8 22.3 %collective-permute-start.26 = (bf16[128,3584]{1,0:T(8,128)(2,1)S(1)}, bf16[128,3584]{1,0:T(8,128)(2,1)S(1)}, u32[]{:S(2)}, u32[]{:S(2)}) collective-permute-start(bf16[128,3584]{1,0:T(8,128)(2,1)S(1)} %bitcast_add_fusion.2), channel_id=1, source_target_pairs={{0,2},{1,3},{2,4},{3,5},{8,10},{9,11},{10,12},{11,13},{16,18},{17,... | collective-permute-start | bytes 2752520 | tf_op jit(solution)/shard_map/ppermute | solution.py:22
  198.5 114.0 %slice-start = ((s8[14680064]{0:T(1024)(128)(4,1)}), s8[2097152]{0:T(1024)(128)(4,1)S(1)}, s32[]{:S(2)}) async-start(s8[14680064]{0:T(1024)(128)(4,1)} %bitcast.173), calls=%async_computation | async-start | bytes 4194304
  198.5 114.0 %slice-start.1 = ((s8[14680064]{0:T(1024)(128)(4,1)}), s8[4194304]{0:T(1024)(128)(4,1)S(1)}, s32[]{:S(2)}) async-start(s8[14680064]{0:T(1024)(128)(4,1)} %bitcast.173), calls=%async_computation.1 | async-start | bytes 8388608
  198.5 114.0 %slice-start.2 = ((s8[14680064]{0:T(1024)(128)(4,1)}), s8[4194304]{0:T(1024)(128)(4,1)S(1)}, s32[]{:S(2)}) async-start(s8[14680064]{0:T(1024)(128)(4,1)} %bitcast.173), calls=%async_computation.2 | async-start | bytes 8388608
  204.0 34.7 %collective-permute-start.18 = (bf16[128,3584]{1,0:T(8,128)(2,1)S(1)}, bf16[128,3584]{1,0:T(8,128)(2,1)S(1)}, u32[]{:S(2)}, u32[]{:S(2)}) collective-permute-start(bf16[128,3584]{1,0:T(8,128)(2,1)S(1)} %bitcast_add_fusion.6), channel_id=1, source_target_pairs={{0,2},{1,3},{2,4},{3,5},{8,10},{9,11},{10,12},{11,13},{16,18},{17,... | collective-permute-start | bytes 2752520 | tf_op jit(solution)/shard_map/ppermute | solution.py:22
  219.2 20.4 %collective-permute-start.29 = (bf16[128,3584]{1,0:T(8,128)(2,1)S(1)}, bf16[128,3584]{1,0:T(8,128)(2,1)S(1)}, u32[]{:S(2)}, u32[]{:S(2)}) collective-permute-start(bf16[128,3584]{1,0:T(8,128)(2,1)S(1)} %get-tuple-element.14), channel_id=1, source_target_pairs={{4,2},{5,3},{6,4},{7,5},{12,10},{13,11},{14,12},{15,13},{20,18},{2... | collective-permute-start | bytes 2752520 | tf_op jit(solution)/shard_map/ppermute | solution.py:22
  219.9 92.6 %slice-start.3 = ((s8[14680064]{0:T(1024)(128)(4,1)}), s8[4194304]{0:T(1024)(128)(4,1)S(1)}, s32[]{:S(2)}) async-start(s8[14680064]{0:T(1024)(128)(4,1)} %bitcast.173), calls=%async_computation.3 | async-start | bytes 8388608
  220.0 38.4 %collective-permute-start.27 = (bf16[128,3584]{1,0:T(8,128)(2,1)S(1)}, bf16[128,3584]{1,0:T(8,128)(2,1)S(1)}, u32[]{:S(2)}, u32[]{:S(2)}) collective-permute-start(bf16[128,3584]{1,0:T(8,128)(2,1)S(1)} %get-tuple-element.13), channel_id=1, source_target_pairs={{0,2},{1,3},{2,4},{3,5},{4,6},{5,7},{8,10},{9,11},{10,12},{11,13},... | collective-permute-start | bytes 2752520 | tf_op jit(solution)/shard_map/ppermute | solution.py:22
  238.9 14.4 %collective-permute-start.21 = (bf16[128,3584]{1,0:T(8,128)(2,1)S(1)}, bf16[128,3584]{1,0:T(8,128)(2,1)S(1)}, u32[]{:S(2)}, u32[]{:S(2)}) collective-permute-start(bf16[128,3584]{1,0:T(8,128)(2,1)S(1)} %get-tuple-element.10), channel_id=1, source_target_pairs={{4,2},{5,3},{6,4},{7,5},{12,10},{13,11},{14,12},{15,13},{20,18},{2... | collective-permute-start | bytes 2752520 | tf_op jit(solution)/shard_map/ppermute | solution.py:22
  239.6 56.6 %collective-permute-start.19 = (bf16[128,3584]{1,0:T(8,128)(2,1)S(1)}, bf16[128,3584]{1,0:T(8,128)(2,1)S(1)}, u32[]{:S(2)}, u32[]{:S(2)}) collective-permute-start(bf16[128,3584]{1,0:T(8,128)(2,1)S(1)} %get-tuple-element.9), channel_id=1, source_target_pairs={{0,2},{1,3},{2,4},{3,5},{4,6},{5,7},{8,10},{9,11},{10,12},{11,13},... | collective-permute-start | bytes 2752520 | tf_op jit(solution)/shard_map/ppermute | solution.py:22
  253.3 40.7 %collective-permute-start.30 = (bf16[128,3584]{1,0:T(8,128)(2,1)S(1)}, bf16[128,3584]{1,0:T(8,128)(2,1)S(1)}, u32[]{:S(2)}, u32[]{:S(2)}) collective-permute-start(bf16[128,3584]{1,0:T(8,128)(2,1)S(1)} %bitcast_add_fusion.1), channel_id=1, source_target_pairs={{2,0},{3,1},{4,2},{5,3},{6,4},{7,5},{10,8},{11,9},{12,10},{13,11},... | collective-permute-start | bytes 2752520 | tf_op jit(solution)/shard_map/ppermute | solution.py:22
  258.3 52.2 %collective-permute-start.22 = (bf16[128,3584]{1,0:T(8,128)(2,1)S(1)}, bf16[128,3584]{1,0:T(8,128)(2,1)S(1)}, u32[]{:S(2)}, u32[]{:S(2)}) collective-permute-start(bf16[128,3584]{1,0:T(8,128)(2,1)S(1)} %bitcast_add_fusion.5), channel_id=1, source_target_pairs={{2,0},{3,1},{4,2},{5,3},{6,4},{7,5},{10,8},{11,9},{12,10},{13,11},... | collective-permute-start | bytes 2752520 | tf_op jit(solution)/shard_map/ppermute | solution.py:22
  294.4 29.6 %collective-permute-start.31 = (bf16[128,3584]{1,0:T(8,128)(2,1)S(1)}, bf16[128,3584]{1,0:T(8,128)(2,1)S(1)}, u32[]{:S(2)}, u32[]{:S(2)}) collective-permute-start(bf16[128,3584]{1,0:T(8,128)(2,1)S(1)} %fusion.53), channel_id=1, source_target_pairs={{8,0},{16,8},{24,16},{0,24},{9,1},{17,9},{25,17},{1,25},{10,2},{18... | collective-permute-start | bytes 2752520 | tf_op jit(solution)/shard_map/ppermute | solution.py:12
  310.9 19.5 %collective-permute-start.23 = (bf16[128,3584]{1,0:T(8,128)(2,1)S(1)}, bf16[128,3584]{1,0:T(8,128)(2,1)S(1)}, u32[]{:S(2)}, u32[]{:S(2)}) collective-permute-start(bf16[128,3584]{1,0:T(8,128)(2,1)S(1)} %fusion.55), channel_id=1, source_target_pairs={{8,0},{16,8},{24,16},{0,24},{9,1},{17,9},{25,17},{1,25},{10,2},{18... | collective-permute-start | bytes 2752520 | tf_op jit(solution)/shard_map/ppermute | solution.py:12

commit v2 on v1

--- a/solution.py
+++ b/solution.py
@@ -1,9 +1,18 @@
+import functools
+
 import jax
 import jax.numpy as jnp
 from jax import lax
+from jax.experimental import pallas as pl
+from jax.experimental.pallas import tpu as pltpu
 from jax.sharding import PartitionSpec as P
 
 PARTS = 2
+CHUNK = 1024
+TILE = 256
+RESIDENT = 40 * 2**20
+F32 = jnp.float32
+BF16 = jnp.bfloat16
 
 
 def shifted(block, axis, distance):
@@ -43,7 +52,7 @@
     return jnp.concatenate([grad_gate, grad_up], axis=-1).astype(jnp.bfloat16)
 
 
-def shards(prev_out, fwd_experts, expert_weights, bwd_experts, grad_hidden, saved_pre):
+def permute_form(prev_out, fwd_experts, expert_weights, bwd_experts, grad_hidden, saved_pre):
     groups = lax.axis_size("ep")
     chips = groups // 2
     capacity = grad_hidden.shape[3]
@@ -141,6 +150,442 @@
     return hidden[None, None], jnp.concatenate(grad_rows, axis=1)[None]
 
 
+def dot(a, b, dims):
+    return lax.dot_general(a, b, (dims, ((), ())), preferred_element_type=F32)
+
+
+def relay_kernel(
+    chunk, routes, prev_out, weights, upstream, saved, hidden, grad_rows,
+    rows, terms, landed, picked, picked_in, part_out, part_own, part_in, result,
+    total, grad_pre, w_fwd, w_bwd, tables, pick_fwd, pick_bwd,
+    shift_send, rows_recv, rows_send, land_recv, land_send, back_send, back_recv,
+    picked_send, picked_recv, part_send, part_recv, wf_sem, wb_sem, table_send, table_recv,
+):
+    chips, _, capacity, hid_units = upstream.shape
+    tokens, width = prev_out.shape
+    count = width // chunk
+    tiles = chunk // TILE
+    sections = lax.axis_size("pp")
+    me, section = lax.axis_index("ep"), lax.axis_index("pp")
+    z, core = me // 2, me % 2
+    other = 1 - core
+    partner = {"ep": 2 * z + other}
+    above = {"ep": jnp.minimum(me + 2, 2 * chips - 1)}
+    below = {"ep": jnp.maximum(me - 2, 0)}
+    after = {"pp": lax.rem(section + 1, sections)}
+    before = {"pp": lax.rem(section + sections - 1, sections)}
+    last = chips - 1
+
+    def remote(src, dst, send, recv, device):
+        return pltpu.make_async_remote_copy(
+            src_ref=src, dst_ref=dst, send_sem=send, recv_sem=recv,
+            device_id=device, device_id_type=pl.DeviceIdType.MESH,
+        )
+
+    def columns(k):
+        return pl.ds(pl.multiple_of(k * chunk, chunk), chunk)
+
+    def tile(i):
+        return pl.ds(pl.multiple_of(i * TILE, TILE), TILE)
+
+    def shift(k):
+        return remote(
+            prev_out.at[:, columns(k)], rows.at[k, z], shift_send.at[k], rows_recv.at[k, z], after
+        )
+
+    def row_up(k, o):
+        return remote(rows.at[k, o], rows.at[k, o], rows_send.at[k, o], rows_recv.at[k, o], above)
+
+    def row_down(k, o):
+        slot = jnp.where(o == z, chips, o)
+        return remote(
+            rows.at[k, o], rows.at[k, o], rows_send.at[k, slot], rows_recv.at[k, o], below
+        )
+
+    def sum_up(k, d):
+        return remote(
+            terms.at[k, d], landed.at[k, d], land_send.at[k, d], land_recv.at[k, d], above
+        )
+
+    def sum_down(k, d):
+        slot = jnp.where(d == z - 1, chips, d)
+        return remote(
+            terms.at[k, d], landed.at[k, slot], land_send.at[k, d], land_recv.at[k, slot], below
+        )
+
+    def landing(k, slot):
+        return remote(
+            terms.at[k, 0], landed.at[k, slot], land_send.at[k, 0], land_recv.at[k, slot], partner
+        )
+
+    def back(k):
+        return remote(
+            result.at[k], grad_rows.at[:, columns(k)], back_send.at[k], back_recv.at[k], before
+        )
+
+    def part_copy(k):
+        s = lax.rem(k, 2)
+        return remote(part_out.at[s], part_in.at[s], part_send.at[s], part_recv.at[s], partner)
+
+    def picked_copy(k):
+        s = lax.rem(k, 2)
+        return remote(
+            picked.at[s], picked_in.at[s], picked_send.at[s], picked_recv.at[s], partner
+        )
+
+    def table_copy(o):
+        return remote(
+            tables.at[z], tables.at[z], table_send.at[o], table_recv.at[z], {"ep": 2 * o + core}
+        )
+
+    def load_fwd(k):
+        s = lax.rem(k, 2)
+        return pltpu.make_async_copy(weights.at[columns(k)], w_fwd.at[s], wf_sem.at[s])
+
+    def load_bwd(k):
+        s = lax.rem(k, 2)
+        return pltpu.make_async_copy(weights.at[columns(k)], w_bwd.at[s], wb_sem.at[s])
+
+    load_bwd(0).start()
+    load_fwd(0).start()
+
+    barrier = pltpu.get_barrier_semaphore()
+    for device in (partner, after, before):
+        pl.semaphore_signal(barrier, 1, device_id=device, device_id_type=pl.DeviceIdType.MESH)
+    for o in range(chips):
+        @pl.when(o != z)
+        def _():
+            pl.semaphore_signal(
+                barrier, 1, device_id={"ep": 2 * o + core}, device_id_type=pl.DeviceIdType.MESH
+            )
+
+    experts = lax.broadcasted_iota(jnp.int32, (chips, tokens), 0)
+    named = jnp.concatenate(
+        [
+            jnp.where(
+                (routes[2 * i : 2 * i + 1, :] == experts)
+                | (routes[2 * i + 1 : 2 * i + 2, :] == experts),
+                1.0,
+                0.0,
+            )
+            for i in range(2)
+        ],
+        axis=0,
+    ).astype(F32)
+    upto = jnp.where(
+        lax.broadcasted_iota(jnp.int32, (tokens, tokens), 0)
+        <= lax.broadcasted_iota(jnp.int32, (tokens, tokens), 1),
+        1.0,
+        0.0,
+    ).astype(BF16)
+    ordinal = dot(named.astype(BF16), upto, ((1,), (0,)))
+    tables[z] = jnp.where(named > 0.5, ordinal - 1.0, -1.0)
+
+    pl.semaphore_wait(barrier, 3 + last)
+    for o in range(chips):
+        @pl.when(o != z)
+        def _():
+            table_copy(o).start()
+    lax.fori_loop(0, count, lambda k, c: (shift(k).start(), c)[1], 0)
+
+    for parity, source in ((0, core), (1, other)):
+        @pl.loop(0, chips)
+        def _(o):
+            gate = saved[o, source, :, :hid_units].astype(F32)
+            up = saved[o, source, :, hid_units:].astype(F32)
+            grad = upstream[o, source].astype(F32)
+            sig = 1.0 / (1.0 + jnp.exp(-gate))
+            grad_pre[parity, o, :, :hid_units] = (
+                grad * up * sig * (1.0 + gate * (1.0 - sig))
+            ).astype(BF16)
+            grad_pre[parity, o, :, hid_units:] = (grad * gate * sig).astype(BF16)
+
+    total[...] = jnp.zeros_like(total)
+
+    for o in range(chips):
+        @pl.when(o != z)
+        def _():
+            remote(
+                tables.at[o], tables.at[o], table_send.at[o], table_recv.at[o], partner
+            ).wait_recv()
+    slots = lax.broadcasted_iota(jnp.int32, (capacity, tokens), 0).astype(F32)
+    for o in range(chips):
+        pick_fwd[o] = jnp.where(tables[o, pl.ds(z, 1), :] == slots, 1.0, 0.0).astype(BF16)
+        pick_bwd[o] = jnp.where(tables[o, pl.ds(chips + z, 1), :] == slots, 1.0, 0.0).astype(BF16)
+
+    def partial_rows(parity, s, target):
+        @pl.loop(0, tiles)
+        def _(i):
+            grads = grad_pre[parity].reshape(chips * capacity, 2 * hid_units)
+            product = dot(grads, w_bwd[s, tile(i), :], ((1,), (1,)))
+            target[:, :, tile(i)] = product.astype(BF16).reshape(chips, capacity, TILE)
+
+    def project(which, source, s):
+        @pl.loop(0, 2 * hid_units // TILE)
+        def _(i):
+            data = source[...].reshape(chips * capacity, chunk)
+            total[which, :, tile(i)] += dot(data, w_fwd[s, :, tile(i)], ((1,), (0,)))
+
+    def add_landed(k, d):
+        terms[k, d] = (terms[k, d].astype(F32) + landed[k, d].astype(F32)).astype(BF16)
+
+    def step(t, carry):
+        @pl.when(t < count)
+        def _():
+            s = lax.rem(t, 2)
+            load_bwd(t).wait()
+
+            @pl.when(t + 1 < count)
+            def _():
+                load_bwd(t + 1).start()
+
+            @pl.when(t >= 2)
+            def _():
+                part_copy(t).wait_send()
+
+            partial_rows(1, s, part_out.at[s])
+            part_copy(t).start()
+            shift(t).wait_recv()
+
+            @pl.when(z < last)
+            def _():
+                row_up(t, z).start()
+
+            @pl.when(z > 0)
+            def _():
+                row_down(t, z).start()
+
+            partial_rows(0, s, part_own)
+            part_copy(t).wait_recv()
+
+            @pl.loop(0, chips)
+            def _(o):
+                @pl.loop(0, tiles)
+                def _(i):
+                    pair = (
+                        part_own[o, :, tile(i)].astype(F32) + part_in[s, o, :, tile(i)].astype(F32)
+                    ).astype(BF16)
+                    terms[t, o, :, tile(i)] = dot(pick_bwd[o], pair, ((0,), (0,))).astype(BF16)
+
+        up_k = t - z
+
+        @pl.when((up_k >= 0) & (up_k < count) & (z < last))
+        def _():
+            for d in range(last, 0, -1):
+                @pl.when(d > z)
+                def _():
+                    @pl.when(z > 0)
+                    def _():
+                        landing(up_k, d).wait_recv()
+                        add_landed(up_k, d)
+
+                    sum_up(up_k, d).start()
+
+        down_k = t - (last - z)
+
+        @pl.when((down_k >= 0) & (down_k < count) & (z > 0))
+        def _():
+            for d in range(last):
+                @pl.when(d < z)
+                def _():
+                    @pl.when(z < last)
+                    def _():
+                        landing(down_k, d).wait_recv()
+                        add_landed(down_k, d)
+
+                    sum_down(down_k, d).start()
+
+        for hop in range(1, chips):
+            k = t - hop
+
+            @pl.when((k >= 0) & (k < count))
+            def _():
+                @pl.when(z >= hop)
+                def _():
+                    o = jnp.maximum(z - hop, 0)
+                    row_up(k, o).wait_recv()
+
+                    @pl.when(z < last)
+                    def _():
+                        row_up(k, o).start()
+
+                @pl.when(z + hop <= last)
+                def _():
+                    o = jnp.minimum(z + hop, last)
+                    row_down(k, o).wait_recv()
+
+                    @pl.when(z > 0)
+                    def _():
+                        row_down(k, o).start()
+
+        end_k = t - last
+
+        @pl.when((end_k >= 0) & (end_k < count))
+        def _():
+            result[end_k] = terms[end_k, z]
+
+            @pl.when(z > 0)
+            def _():
+                landing(end_k, z).wait_recv()
+                result[end_k] = (
+                    result[end_k].astype(F32) + landed[end_k, z].astype(F32)
+                ).astype(BF16)
+
+            @pl.when(z < last)
+            def _():
+                landing(end_k, chips).wait_recv()
+                result[end_k] = (
+                    result[end_k].astype(F32) + landed[end_k, chips].astype(F32)
+                ).astype(BF16)
+
+            back(end_k).start()
+
+        mul_k = t - chips
+
+        @pl.when((mul_k >= 0) & (mul_k < count))
+        def _():
+            s = lax.rem(mul_k, 2)
+            load_fwd(mul_k).wait()
+
+            @pl.when(mul_k + 1 < count)
+            def _():
+                load_fwd(mul_k + 1).start()
+
+            project(0, picked.at[s], s)
+            picked_copy(mul_k).wait()
+            project(1, picked_in.at[s], s)
+
+        @pl.when((end_k >= 0) & (end_k < count))
+        def _():
+            s = lax.rem(end_k, 2)
+
+            @pl.loop(0, chips)
+            def _(o):
+                @pl.loop(0, tiles)
+                def _(i):
+                    picked[s, o, :, tile(i)] = dot(
+                        pick_fwd[o], rows[end_k, o, :, tile(i)], ((1,), (0,))
+                    ).astype(BF16)
+
+            picked_copy(end_k).start()
+
+        return carry
+
+    lax.fori_loop(0, count + chips, step, 0)
+
+    for parity, source in ((0, core), (1, other)):
+        @pl.loop(0, chips)
+        def _(o):
+            block = pl.ds(pl.multiple_of(o * capacity, capacity), capacity)
+            gate = total[parity, block, :hid_units]
+            up = total[parity, block, hid_units:]
+            hidden[o, source] = (gate / (1.0 + jnp.exp(-gate)) * up).astype(BF16)
+
+    def finish(k, carry):
+        shift(k).wait_send()
+        back(k).wait()
+        for o in range(chips):
+            @pl.when((o <= z) & (z < last))
+            def _():
+                row_up(k, o).wait_send()
+
+            @pl.when((o >= z) & (z > 0))
+            def _():
+                row_down(k, o).wait_send()
+
+            @pl.when(o != z)
+            def _():
+                sum_up(k, o).wait_send()
+
+        return carry
+
+    lax.fori_loop(0, count, finish, 0)
+    for k in range(max(count - 2, 0), count):
+        part_copy(k).wait_send()
+    for o in range(chips):
+        @pl.when(o != z)
+        def _():
+            table_copy(o).wait_send()
+
+
+def kernel_form(prev_out, fwd_experts, expert_weights, bwd_experts, grad_hidden, saved_pre):
+    groups, capacity, hid_units = grad_hidden.shape[2:]
+    chips = groups // 2
+    tokens, width = prev_out.shape[1:]
+    chunk = CHUNK
+    count = width // chunk
+    routes = jnp.concatenate([fwd_experts[0], bwd_experts[0]], axis=1).T
+    hbm = pl.BlockSpec(memory_space=pl.ANY)
+    vmem = pl.BlockSpec(memory_space=pltpu.VMEM)
+    dma = pltpu.SemaphoreType.DMA
+    slots = chips * capacity
+    hidden, grad_rows = pl.pallas_call(
+        functools.partial(relay_kernel, chunk),
+        out_shape=(
+            jax.ShapeDtypeStruct((chips, 2, capacity, hid_units), BF16),
+            jax.ShapeDtypeStruct((tokens, width), BF16),
+        ),
+        in_specs=[vmem, hbm, hbm, vmem, vmem],
+        out_specs=(vmem, hbm),
+        scratch_shapes=[
+            pltpu.VMEM((count, chips, tokens, chunk), BF16),
+            pltpu.VMEM((count, chips, tokens, chunk), BF16),
+            pltpu.VMEM((count, chips + 1, tokens, chunk), BF16),
+            pltpu.VMEM((2, chips, capacity, chunk), BF16),
+            pltpu.VMEM((2, chips, capacity, chunk), BF16),
+            pltpu.VMEM((2, chips, capacity, chunk), BF16),
+            pltpu.VMEM((chips, capacity, chunk), BF16),
+            pltpu.VMEM((2, chips, capacity, chunk), BF16),
+            pltpu.VMEM((count, tokens, chunk), BF16),
+            pltpu.VMEM((2, slots, 2 * hid_units), F32),
+            pltpu.VMEM((2, chips, capacity, 2 * hid_units), BF16),
+            pltpu.VMEM((2, chunk, 2 * hid_units), BF16),
+            pltpu.VMEM((2, chunk, 2 * hid_units), BF16),
+            pltpu.VMEM((chips, 2 * chips, tokens), F32),
+            pltpu.VMEM((chips, capacity, tokens), BF16),
+            pltpu.VMEM((chips, capacity, tokens), BF16),
+            dma((count,)),
+            dma((count, chips)),
+            dma((count, chips + 1)),
+            dma((count, chips + 1)),
+            dma((count, chips)),
+            dma((count,)),
+            dma((count,)),
+            dma((2,)),
+            dma((2,)),
+            dma((2,)),
+            dma((2,)),
+            dma((2,)),
+            dma((2,)),
+            dma((chips,)),
+            dma((chips,)),
+        ],
+        compiler_params=pltpu.CompilerParams(
+            collective_id=0, has_side_effects=True, vmem_limit_bytes=60 * 2**20
+        ),
+        cost_estimate=pl.CostEstimate(
+            flops=8 * groups * capacity * width * hid_units,
+            bytes_accessed=4 * width * hid_units,
+            transcendentals=2 * groups * capacity * hid_units,
+        ),
+        name="relay",
+    )(
+        routes,
+        prev_out[0],
+        expert_weights[0, 0],
+        grad_hidden.reshape(chips, 2, capacity, hid_units),
+        saved_pre.reshape(chips, 2, capacity, 2 * hid_units),
+    )
+    return hidden.reshape(grad_hidden.shape), grad_rows[None]
+
+
+def shards(prev_out, *rest):
+    chips = lax.axis_size("ep") // 2
+    held = 3 * chips * prev_out.shape[1] * prev_out.shape[2] * 2
+    form = kernel_form if held <= RESIDENT and prev_out.shape[2] % CHUNK == 0 else permute_form
+    return form(prev_out, *rest)
+
+
 def solution(mesh):
     placed = (
         P("pp", "ep", None),

time: 333 us -> 215 us (0.65)
  Pallas kernels: 0 us -> 208 us
  waiting for transfers between devices: 133 us -> 0 us
  starting transfers between devices: 88.8 us -> 0 us
  matrix products: 55 us -> 0 us
  blocking collectives: 26.8 us -> 0 us
  local copies, waits for them, and re-layouts: 16 us -> 4.91 us
  other arithmetic: 10.9 us -> 1.28 us
    pallas_call x0 -> x1, Pallas kernels: none -> 208 us  [kernel_form(): pl.pallas_call(functools.partial(relay_kernel, chunk), out_shape=(jax.Sha...]
    ppermute x32 -> x0, waiting for transfers between devices: 133 us -> none  [the longest x24 92.5 us: step_along(): return lax.ppermute(value, 'ep', pairs)]
    ppermute x32 -> x0, starting transfers between devices: 88.8 us -> none  [the longest x24 80.4 us: step_along(): return lax.ppermute(value, 'ep', pairs)]
    dot_general x10 -> x0, matrix products: 55 us -> none  [the longest x2 19.7 us: shards(): jnp.einsum('nct,ncd->ntd', bwd_own, pair, preferred_element_type=jnp.floa...]
    all_gather x1 -> x0, blocking collectives: 26.8 us -> none  [shards(): lax.all_gather(jnp.concatenate([fwd_experts[0], bwd_experts[0]], axis=1),...]
    unnamed x41 -> x2, local copies, waits for them, and re-layouts: 10.3 us -> 4.91 us
    another operation x6 -> x0, other arithmetic: 4.96 us -> none  [the longest x2 2.45 us: slots_of(): slot = jnp.cumsum(named, axis=1) - 1]
    squeeze x3 -> x0, local copies, waits for them, and re-layouts: 4.65 us -> none  [the longest x2 4.53 us: shards(): lax.dynamic_index_in_dim(terms, jnp.minimum(z + chips - hop, chips - 1),...]
  transfers between devices with their start and end apart: 32 -> 0, of which waited for: 10 -> 0; matrix products, arithmetic and copies ran while one was open for 21% -> 0% of each run, Pallas kernels for 0% -> 0%
where the time goes in v2:
time: 215 us
  Pallas kernels  208 us (97%)
  local copies, waits for them, and re-layouts  4.91 us (2%)
    pallas_call x1, Pallas kernels, kernel_form(): pl.pallas_call(functools.partial(relay_kernel, chunk), out_shape=(jax.Sha...  208 us
    unnamed x2, local copies, waits for them, and re-layouts  4.91 us

profile of v2, /device:TPU:0, one launch (start us, length us, event | category | flops | bytes accessed | tf_op | source)
XLA Modules:
  0.0 215.1 jit_solution(7641142141516841251)
XLA Ops:
  0.6 1.3 add_bitcast_fusion.routes
  1.9 208.2 %relay.1 = (bf16[4,2,96,512]{3,2,1,0:T(8,128)(2,1)}, bf16[128,7168]{1,0:T(8,128)(2,1)}) custom-call(s32[4,128]{1,0:T(4,128)} %add_bitcast_fusion.routes, bf16[128,7168]{1,0:T(8,128)(2,1)} %bitcast.15, bf16[7168,1024]{1,0:T(8,128)(2,1)} %bitcast.14, bf16[4,2,96,512]{3,2,1,0:T(8,128)(2,1)} %bitcast.17, bf16[4,2,96,1024]{3,2,1,0:T(8,128)(2,1)} %bitcast.16), custom_call_target="tpu_custom_call" | custom-call | flops 22548578304 | bytes 14680064 | tf_op jit(solution)/shard_map/relay/pallas_call | solution.py:522
  210.2 2.1 copy.10
  212.2 2.8 %copy.11 = bf16[1,128,7168]{2,1,0:T(8,128)(2,1)} copy(bf16[1,128,7168]{2,1,0:T(8,128)(2,1)} %bitcast.10) | data formatting | bytes 3670016

commit v3 on v2

--- a/solution.py
+++ b/solution.py
@@ -8,7 +8,7 @@
 from jax.sharding import PartitionSpec as P
 
 PARTS = 2
-CHUNK = 1024
+CHUNK = 512
 TILE = 256
 RESIDENT = 40 * 2**20
 F32 = jnp.float32

time: 215 us -> 203 us (0.944)
  Pallas kernels: 208 us -> 196 us
    pallas_call x1, Pallas kernels: 208 us -> 196 us  [kernel_form(): pl.pallas_call(functools.partial(relay_kernel, chunk), out_shape=(jax.Sha...]
where the time goes in v3:
time: 203 us
  Pallas kernels  196 us (97%)
  local copies, waits for them, and re-layouts  4.91 us (2%)
    pallas_call x1, Pallas kernels, kernel_form(): pl.pallas_call(functools.partial(relay_kernel, chunk), out_shape=(jax.Sha...  196 us
    unnamed x2, local copies, waits for them, and re-layouts  4.91 us

profile of v3, /device:TPU:0, one launch (start us, length us, event | category | flops | bytes accessed | tf_op | source)
XLA Modules:
  0.0 202.8 jit_solution(16618624739323827423)
XLA Ops:
  0.6 1.3 add_bitcast_fusion.routes
  1.9 196.0 %relay.1 = (bf16[4,2,96,512]{3,2,1,0:T(8,128)(2,1)}, bf16[128,7168]{1,0:T(8,128)(2,1)}) custom-call(s32[4,128]{1,0:T(4,128)} %add_bitcast_fusion.routes, bf16[128,7168]{1,0:T(8,128)(2,1)} %bitcast.15, bf16[7168,1024]{1,0:T(8,128)(2,1)} %bitcast.14, bf16[4,2,96,512]{3,2,1,0:T(8,128)(2,1)} %bitcast.17, bf16[4,2,96,1024]{3,2,1,0:T(8,128)(2,1)} %bitcast.16), custom_call_target="tpu_custom_call" | custom-call | flops 22548578304 | bytes 14680064 | tf_op jit(solution)/shard_map/relay/pallas_call | solution.py:522
  197.9 2.1 %copy.10 = bf16[1,1,8,96,512]{4,3,2,1,0:T(8,128)(2,1)} copy(bf16[1,1,8,96,512]{4,3,2,1,0:T(8,128)(2,1)} %bitcast.11) | data formatting | bytes 1572864
  200.0 2.8 %copy.11 = bf16[1,128,7168]{2,1,0:T(8,128)(2,1)} copy(bf16[1,128,7168]{2,1,0:T(8,128)(2,1)} %bitcast.10) | data formatting | bytes 3670016

commit v4 on v3

--- a/solution.py
+++ b/solution.py
@@ -9,6 +9,7 @@
 
 PARTS = 2
 CHUNK = 512
+EARLY = 2
 TILE = 256
 RESIDENT = 40 * 2**20
 F32 = jnp.float32
@@ -288,7 +289,23 @@
             table_copy(o).start()
     lax.fori_loop(0, count, lambda k, c: (shift(k).start(), c)[1], 0)
 
-    for parity, source in ((0, core), (1, other)):
+    early = min(EARLY, count)
+
+    def send_own(k):
+        shift(k).wait_recv()
+
+        @pl.when(z < last)
+        def _():
+            row_up(k, z).start()
+
+        @pl.when(z > 0)
+        def _():
+            row_down(k, z).start()
+
+    for parity, source in ((1, other), (0, core)):
+        if 1 - parity < early:
+            send_own(1 - parity)
+
         @pl.loop(0, chips)
         def _(o):
             gate = saved[o, source, :, :hid_units].astype(F32)
@@ -329,10 +346,48 @@
     def add_landed(k, d):
         terms[k, d] = (terms[k, d].astype(F32) + landed[k, d].astype(F32)).astype(BF16)
 
+    def hop_rows(t, hop):
+        k = t - hop
+
+        @pl.when((k >= 0) & (k < count))
+        def _():
+            @pl.when(z >= hop)
+            def _():
+                o = jnp.maximum(z - hop, 0)
+                row_up(k, o).wait_recv()
+
+                @pl.when(z < last)
+                def _():
+                    row_up(k, o).start()
+
+            @pl.when(z + hop <= last)
+            def _():
+                o = jnp.minimum(z + hop, last)
+                row_down(k, o).wait_recv()
+
+                @pl.when(z > 0)
+                def _():
+                    row_down(k, o).start()
+
+    def sum_on(k, d, first, copy):
+        @pl.when((k >= 0) & (k < count))
+        def _():
+            @pl.when(jnp.logical_not(first))
+            def _():
+                landing(k, d).wait_recv()
+                add_landed(k, d)
+
+            copy(k, d).start()
+
     def step(t, carry):
         @pl.when(t < count)
         def _():
             s = lax.rem(t, 2)
+
+            @pl.when(t >= early)
+            def _():
+                send_own(t)
+
             load_bwd(t).wait()
 
             @pl.when(t + 1 < count)
@@ -345,17 +400,13 @@
 
             partial_rows(1, s, part_out.at[s])
             part_copy(t).start()
-            shift(t).wait_recv()
-
-            @pl.when(z < last)
-            def _():
-                row_up(t, z).start()
-
-            @pl.when(z > 0)
-            def _():
-                row_down(t, z).start()
-
             partial_rows(0, s, part_own)
+
+        hop_rows(t, 1)
+
+        @pl.when(t < count)
+        def _():
+            s = lax.rem(t, 2)
             part_copy(t).wait_recv()
 
             @pl.loop(0, chips)
@@ -367,56 +418,26 @@
                     ).astype(BF16)
                     terms[t, o, :, tile(i)] = dot(pick_bwd[o], pair, ((0,), (0,))).astype(BF16)
 
-        up_k = t - z
-
-        @pl.when((up_k >= 0) & (up_k < count) & (z < last))
-        def _():
-            for d in range(last, 0, -1):
-                @pl.when(d > z)
-                def _():
-                    @pl.when(z > 0)
-                    def _():
-                        landing(up_k, d).wait_recv()
-                        add_landed(up_k, d)
-
-                    sum_up(up_k, d).start()
-
-        down_k = t - (last - z)
-
-        @pl.when((down_k >= 0) & (down_k < count) & (z > 0))
-        def _():
-            for d in range(last):
-                @pl.when(d < z)
-                def _():
-                    @pl.when(z < last)
-                    def _():
-                        landing(down_k, d).wait_recv()
-                        add_landed(down_k, d)
-
-                    sum_down(down_k, d).start()
-
-        for hop in range(1, chips):
-            k = t - hop
-
-            @pl.when((k >= 0) & (k < count))
-            def _():
-                @pl.when(z >= hop)
-                def _():
-                    o = jnp.maximum(z - hop, 0)
-                    row_up(k, o).wait_recv()
-
-                    @pl.when(z < last)
-                    def _():
-                        row_up(k, o).start()
-
-                @pl.when(z + hop <= last)
-                def _():
-                    o = jnp.minimum(z + hop, last)
-                    row_down(k, o).wait_recv()
-
-                    @pl.when(z > 0)
-                    def _():
-                        row_down(k, o).start()
+        for hop in range(2, chips):
+            hop_rows(t, hop)
+
+        for d in range(last, 0, -1):
+            @pl.when(d > z + 1)
+            def _():
+                sum_on(t - z, d, z == 0, sum_up)
+
+        for d in range(last):
+            @pl.when(d < z - 1)
+            def _():
+                sum_on(t - last + z, d, z == last, sum_down)
+
+        @pl.when(z < last)
+        def _():
+            sum_on(t - last + 1, jnp.minimum(z + 1, last), z == 0, sum_up)
+
+        @pl.when(z > 0)
+        def _():
+            sum_on(t - last + 1, jnp.maximum(z - 1, 0), z == last, sum_down)
 
         end_k = t - last
 

time: 203 us -> 198 us (0.975)
  Pallas kernels: 196 us -> 191 us
    pallas_call x1, Pallas kernels: 196 us -> 191 us  [kernel_form(): pl.pallas_call(functools.partial(relay_kernel, chunk), out_shape=(jax.Sha...]
where the time goes in v4:
time: 198 us
  Pallas kernels  191 us (96%)
  local copies, waits for them, and re-layouts  4.91 us (2%)
    pallas_call x1, Pallas kernels, kernel_form(): pl.pallas_call(functools.partial(relay_kernel, chunk), out_shape=(jax.Sha...  191 us
    unnamed x2, local copies, waits for them, and re-layouts  4.91 us

profile of v4, /device:TPU:0, one launch (start us, length us, event | category | flops | bytes accessed | tf_op | source)
XLA Modules:
  0.0 197.9 jit_solution(10302302412524928045)
XLA Ops:
  0.6 1.3 add_bitcast_fusion.routes
  1.9 191.1 %relay.1 = (bf16[4,2,96,512]{3,2,1,0:T(8,128)(2,1)}, bf16[128,7168]{1,0:T(8,128)(2,1)}) custom-call(s32[4,128]{1,0:T(4,128)} %add_bitcast_fusion.routes, bf16[128,7168]{1,0:T(8,128)(2,1)} %bitcast.15, bf16[7168,1024]{1,0:T(8,128)(2,1)} %bitcast.14, bf16[4,2,96,512]{3,2,1,0:T(8,128)(2,1)} %bitcast.17, bf16[4,2,96,1024]{3,2,1,0:T(8,128)(2,1)} %bitcast.16), custom_call_target="tpu_custom_call" | custom-call | flops 22548578304 | bytes 14680064 | tf_op jit(solution)/shard_map/relay/pallas_call | solution.py:543
  193.0 2.1 %copy.10 = bf16[1,1,8,96,512]{4,3,2,1,0:T(8,128)(2,1)} copy(bf16[1,1,8,96,512]{4,3,2,1,0:T(8,128)(2,1)} %bitcast.11) | data formatting | bytes 1572864
  195.1 2.8 %copy.11 = bf16[1,128,7168]{2,1,0:T(8,128)(2,1)} copy(bf16[1,128,7168]{2,1,0:T(8,128)(2,1)} %bitcast.10) | data formatting | bytes 3670016

commit v5 on v4

--- a/solution.py
+++ b/solution.py
@@ -8,8 +8,7 @@
 from jax.sharding import PartitionSpec as P
 
 PARTS = 2
-CHUNK = 512
-EARLY = 2
+CHUNK = 256
 TILE = 256
 RESIDENT = 40 * 2**20
 F32 = jnp.float32
@@ -289,7 +288,7 @@
             table_copy(o).start()
     lax.fori_loop(0, count, lambda k, c: (shift(k).start(), c)[1], 0)
 
-    early = min(EARLY, count)
+    early = min(chips, count)
 
     def send_own(k):
         shift(k).wait_recv()
@@ -303,11 +302,13 @@
             row_down(k, z).start()
 
     for parity, source in ((1, other), (0, core)):
-        if 1 - parity < early:
-            send_own(1 - parity)
-
         @pl.loop(0, chips)
         def _(o):
+            if parity:
+                @pl.when(o < early)
+                def _():
+                    send_own(o)
+
             gate = saved[o, source, :, :hid_units].astype(F32)
             up = saved[o, source, :, hid_units:].astype(F32)
             grad = upstream[o, source].astype(F32)

time: 198 us -> 197 us (level)
  no operation moved by 1% of the time
where the time goes in v5:
time: 197 us
  Pallas kernels  190 us (96%)
  local copies, waits for them, and re-layouts  4.91 us (2%)
    pallas_call x1, Pallas kernels, kernel_form(): pl.pallas_call(functools.partial(relay_kernel, chunk), out_shape=(jax.Sha...  190 us
    unnamed x2, local copies, waits for them, and re-layouts  4.91 us

profile of v5, /device:TPU:0, one launch (start us, length us, event | category | flops | bytes accessed | tf_op | source)
XLA Modules:
  0.0 196.8 jit_solution(16235934578256235807)
XLA Ops:
  0.6 1.3 add_bitcast_fusion.routes
  1.9 190.0 %relay.1 = (bf16[4,2,96,512]{3,2,1,0:T(8,128)(2,1)}, bf16[128,7168]{1,0:T(8,128)(2,1)}) custom-call(s32[4,128]{1,0:T(4,128)} %add_bitcast_fusion.routes, bf16[128,7168]{1,0:T(8,128)(2,1)} %bitcast.15, bf16[7168,1024]{1,0:T(8,128)(2,1)} %bitcast.14, bf16[4,2,96,512]{3,2,1,0:T(8,128)(2,1)} %bitcast.17, bf16[4,2,96,1024]{3,2,1,0:T(8,128)(2,1)} %bitcast.16), custom_call_target="tpu_custom_call" | custom-call | flops 22548578304 | bytes 14680064 | tf_op jit(solution)/shard_map/relay/pallas_call | solution.py:544
  191.9 2.1 %copy.10 = bf16[1,1,8,96,512]{4,3,2,1,0:T(8,128)(2,1)} copy(bf16[1,1,8,96,512]{4,3,2,1,0:T(8,128)(2,1)} %bitcast.11) | data formatting | bytes 1572864
  194.0 2.8 %copy.11 = bf16[1,128,7168]{2,1,0:T(8,128)(2,1)} copy(bf16[1,128,7168]{2,1,0:T(8,128)(2,1)} %bitcast.10) | data formatting | bytes 3670016

commit v6 on v5

--- a/solution.py
+++ b/solution.py
@@ -8,7 +8,8 @@
 from jax.sharding import PartitionSpec as P
 
 PARTS = 2
-CHUNK = 256
+CHUNK = 512
+LEAD = 2
 TILE = 256
 RESIDENT = 40 * 2**20
 F32 = jnp.float32
@@ -348,7 +349,7 @@
         terms[k, d] = (terms[k, d].astype(F32) + landed[k, d].astype(F32)).astype(BF16)
 
     def hop_rows(t, hop):
-        k = t - hop
+        k = t + LEAD - hop
 
         @pl.when((k >= 0) & (k < count))
         def _():
@@ -381,14 +382,13 @@
             copy(k, d).start()
 
     def step(t, carry):
-        @pl.when(t < count)
+        @pl.when((t + LEAD >= early) & (t + LEAD < count))
+        def _():
+            send_own(t + LEAD)
+
+        @pl.when((t >= 0) & (t < count))
         def _():
             s = lax.rem(t, 2)
-
-            @pl.when(t >= early)
-            def _():
-                send_own(t)
-
             load_bwd(t).wait()
 
             @pl.when(t + 1 < count)
@@ -405,7 +405,7 @@
 
         hop_rows(t, 1)
 
-        @pl.when(t < count)
+        @pl.when((t >= 0) & (t < count))
         def _():
             s = lax.rem(t, 2)
             part_copy(t).wait_recv()
@@ -462,7 +462,7 @@
 
             back(end_k).start()
 
-        mul_k = t - chips
+        mul_k = t + LEAD - chips
 
         @pl.when((mul_k >= 0) & (mul_k < count))
         def _():
@@ -477,23 +477,25 @@
             picked_copy(mul_k).wait()
             project(1, picked_in.at[s], s)
 
-        @pl.when((end_k >= 0) & (end_k < count))
-        def _():
-            s = lax.rem(end_k, 2)
+        pick_k = mul_k + 1
+
+        @pl.when((pick_k >= 0) & (pick_k < count))
+        def _():
+            s = lax.rem(pick_k, 2)
 
             @pl.loop(0, chips)
             def _(o):
                 @pl.loop(0, tiles)
                 def _(i):
                     picked[s, o, :, tile(i)] = dot(
-                        pick_fwd[o], rows[end_k, o, :, tile(i)], ((1,), (0,))
+                        pick_fwd[o], rows[pick_k, o, :, tile(i)], ((1,), (0,))
                     ).astype(BF16)
 
-            picked_copy(end_k).start()
+            picked_copy(pick_k).start()
 
         return carry
 
-    lax.fori_loop(0, count + chips, step, 0)
+    lax.fori_loop(-LEAD, count + chips, step, 0)
 
     for parity, source in ((0, core), (1, other)):
         @pl.loop(0, chips)

time: 197 us -> 194 us (0.985)
  Pallas kernels: 190 us -> 187 us
    pallas_call x1, Pallas kernels: 190 us -> 187 us  [kernel_form(): pl.pallas_call(functools.partial(relay_kernel, chunk), out_shape=(jax.Sha...]
where the time goes in v6:
time: 194 us; the launch traced here: 193 us
  Pallas kernels  187 us (96%)
  local copies, waits for them, and re-layouts  4.91 us (3%)
    pallas_call x1, Pallas kernels, kernel_form(): pl.pallas_call(functools.partial(relay_kernel, chunk), out_shape=(jax.Sha...  187 us
    unnamed x2, local copies, waits for them, and re-layouts  4.91 us

profile of v6, /device:TPU:0, one launch (start us, length us, event | category | flops | bytes accessed | tf_op | source)
XLA Modules:
  0.0 193.4 jit_solution(4669394440981472882)
XLA Ops:
  0.6 1.3 add_bitcast_fusion.routes
  1.9 186.6 %relay.1 = (bf16[4,2,96,512]{3,2,1,0:T(8,128)(2,1)}, bf16[128,7168]{1,0:T(8,128)(2,1)}) custom-call(s32[4,128]{1,0:T(4,128)} %add_bitcast_fusion.routes, bf16[128,7168]{1,0:T(8,128)(2,1)} %bitcast.15, bf16[7168,1024]{1,0:T(8,128)(2,1)} %bitcast.14, bf16[4,2,96,512]{3,2,1,0:T(8,128)(2,1)} %bitcast.17, bf16[4,2,96,1024]{3,2,1,0:T(8,128)(2,1)} %bitcast.16), custom_call_target="tpu_custom_call" | custom-call | flops 22548578304 | bytes 14680064 | tf_op jit(solution)/shard_map/relay/pallas_call | solution.py:546
  188.5 2.1 %copy.10 = bf16[1,1,8,96,512]{4,3,2,1,0:T(8,128)(2,1)} copy(bf16[1,1,8,96,512]{4,3,2,1,0:T(8,128)(2,1)} %bitcast.11) | data formatting | bytes 1572864
  190.6 2.8 %copy.11 = bf16[1,128,7168]{2,1,0:T(8,128)(2,1)} copy(bf16[1,128,7168]{2,1,0:T(8,128)(2,1)} %bitcast.10) | data formatting | bytes 3670016

commit v7 on v6

--- a/solution.py
+++ b/solution.py
@@ -287,12 +287,16 @@
         @pl.when(o != z)
         def _():
             table_copy(o).start()
-    lax.fori_loop(0, count, lambda k, c: (shift(k).start(), c)[1], 0)
-
     early = min(chips, count)
+    for k in range(early):
+        shift(k).start()
 
     def send_own(k):
         shift(k).wait_recv()
+
+        @pl.when(k + early < count)
+        def _():
+            shift(k + early).start()
 
         @pl.when(z < last)
         def _():

time: 194 us -> 194 us (level)
  no operation moved by 1% of the time
where the time goes in v7:
time: 194 us; the launch traced here: 193 us
  Pallas kernels  187 us (96%)
  local copies, waits for them, and re-layouts  4.91 us (3%)
    pallas_call x1, Pallas kernels, kernel_form(): pl.pallas_call(functools.partial(relay_kernel, chunk), out_shape=(jax.Sha...  187 us
    unnamed x2, local copies, waits for them, and re-layouts  4.91 us

profile of v7, /device:TPU:0, one launch (start us, length us, event | category | flops | bytes accessed | tf_op | source)
XLA Modules:
  0.0 193.4 jit_solution(919815225333485534)
XLA Ops:
  0.6 1.3 add_bitcast_fusion.routes
  1.9 186.6 %relay.1 = (bf16[4,2,96,512]{3,2,1,0:T(8,128)(2,1)}, bf16[128,7168]{1,0:T(8,128)(2,1)}) custom-call(s32[4,128]{1,0:T(4,128)} %add_bitcast_fusion.routes, bf16[128,7168]{1,0:T(8,128)(2,1)} %bitcast.15, bf16[7168,1024]{1,0:T(8,128)(2,1)} %bitcast.14, bf16[4,2,96,512]{3,2,1,0:T(8,128)(2,1)} %bitcast.17, bf16[4,2,96,1024]{3,2,1,0:T(8,128)(2,1)} %bitcast.16), custom_call_target="tpu_custom_call" | custom-call | flops 22548578304 | bytes 14680064 | tf_op jit(solution)/shard_map/relay/pallas_call | solution.py:550
  188.5 2.1 %copy.10 = bf16[1,1,8,96,512]{4,3,2,1,0:T(8,128)(2,1)} copy(bf16[1,1,8,96,512]{4,3,2,1,0:T(8,128)(2,1)} %bitcast.11) | data formatting | bytes 1572864
  190.6 2.8 %copy.11 = bf16[1,128,7168]{2,1,0:T(8,128)(2,1)} copy(bf16[1,128,7168]{2,1,0:T(8,128)(2,1)} %bitcast.10) | data formatting | bytes 3670016
